TPU v7x, 32 devices: a whole 2x2x4 slice. The times are simulated.
32 devices in a mesh: dp: 8 (over z, x), group: 4 (over y, core).
Axes of the slice: x: 2, y: 2, z: 4, core: 2. Of those that a mesh axis runs over, the one named last changes fastest.
Arguments:
- inputs: bfloat16 [32, 256, 512], P(('dp', 'group')), may hold values from -6 to 6
- cotangent: bfloat16 [32, 256, 512], P(('dp', 'group')), may hold values from -6 to 6
- lengths: int32 [32], replicated, may hold values from 48 to 256, as said below
- square_slots: int32 [16], replicated, may hold values from 0 to 15, each once
- wide_slots: int32 [8], replicated, may hold values from 0 to 7, each once
- square_weights: bfloat16 [16, 512, 512], P('group'), may hold values from -0.25 to 0.25
- wide_weights: bfloat16 [8, 512, 2048], P('group'), may hold values from -0.25 to 0.25
- vectors: float32 [2, 48, 512], P(None, 'group'), may hold values from -1.5 to 1.5
- square_moment: float32 [16, 512, 512], P('group'), may hold values from -160 to 160
- wide_moment: float32 [8, 512, 2048], P('group'), may hold values from -160 to 160
- vector_moment: float32 [2, 48, 512], P(None, 'group'), may hold values from -28 to 28
- vector_second: float32 [2, 48, 512], P(None, 'group'), may hold values from 20.48 to 81.92
Outputs:
- block_output: bfloat16 [32, 256, 512], P(('dp', 'group'))
- input_grad: float32 [32, 256, 512], P(('dp', 'group'))
- square_moment_new: float32 [16, 512, 512], P('group')
- square_new: float32 [16, 512, 512], P('group')
- wide_moment_new: float32 [8, 512, 2048], P('group')
- wide_new: float32 [8, 512, 2048], P('group')
- vector_moment_new: float32 [2, 48, 512], P(None, 'group')
- vector_second_new: float32 [2, 48, 512], P(None, 'group')
- vector_new: float32 [2, 48, 512], P(None, 'group')
Inputs may be any that keep to these rules, and one draw needn't show every extreme that they name: `lengths`: the last sequence has all 256 positions valid.
All inputs are finite; a program needn't handle non-finite values.
Results may differ from a plain program's by a relative error of at most 0.035.
Values may be sent and summed in bfloat16 or wider, within the bound.
A program may use at most 320 MiB of HBM per device.

v0:
```python
from functools import partial
import math

import jax
import jax.numpy as jnp
from jax import lax
from jax.sharding import PartitionSpec as P

D = 512
HEADS = 8
HEAD_DIM = 64
LAYERS = 2
NS_ITERS = 5
STEP = 10
SQUARES = 16
WIDES = 8


norm_epsilon = 1e-05
quintic_first = 3.4445
quintic_second = -4.775
quintic_third = 2.0315
momentum_decay = 0.95
muon_rate = 0.1
weight_decay = 0.01
adam_first = 0.9
adam_second = 0.99
adam_rate = 0.3
adam_epsilon = 1e-08


def layer_norm(x, gain, shift):
    middle = jnp.mean(x, -1, keepdims=True)
    centred = x - middle
    spread = jnp.mean(centred * centred, -1, keepdims=True)
    return centred * lax.rsqrt(spread + norm_epsilon) * gain + shift


def masked_norm(x, gain, shift, mask):
    return layer_norm(x, gain, shift) * mask


def rel_table(rows, width):
    offset = (rows - 1 - jnp.arange(2 * rows)).astype(jnp.float32)
    freq = jnp.exp(jnp.arange(0, width, 2).astype(jnp.float32) * (-math.log(10000.0) / width))
    angle = offset[:, None] * freq[None, :]
    return jnp.stack([jnp.sin(angle), jnp.cos(angle)], axis=-1).reshape(2 * rows, width)


def shift_rel(full):
    heads, rows, cols = full.shape
    flat = full.reshape(heads, rows * cols)
    flat = flat[:, rows - 1 : rows - 1 + rows * (cols - 1)]
    return flat.reshape(heads, rows, cols - 1)[:, :, :rows]


def unshift_rel(part_grad):
    heads, rows, _ = part_grad.shape
    widened = jnp.pad(part_grad, ((0, 0), (0, 0), (0, rows - 1)))
    flat = widened.reshape(heads, rows * (2 * rows - 1))
    flat = jnp.pad(flat, ((0, 0), (rows - 1, 1)))
    return flat.reshape(heads, rows, 2 * rows)


def depthwise(glu, kernel):
    width = kernel.shape[0]
    half = width // 2
    rows = glu.shape[0]
    padded = jnp.pad(glu, ((half, half), (0, 0)))
    total = jnp.zeros_like(glu)
    for tap in range(width):
        total = total + padded[tap : tap + rows] * kernel[tap]
    return total


def product(left, right):
    return jnp.dot(left, right, preferred_element_type=jnp.float32)


def cross_rows(left, right):
    return lax.dot_general(
        left, right, (((0,), (0,)), ((), ())), preferred_element_type=jnp.float32
    )


def cross_cols(left, right):
    return lax.dot_general(
        left, right, (((1,), (1,)), ((), ())), preferred_element_type=jnp.float32
    )


def split_heads(value):
    return value.reshape(value.shape[0], HEADS, -1)


def silu_slope(value):
    sig = jax.nn.sigmoid(value)
    return sig * (1.0 + value * (1.0 - sig))


def feed_forward(x, gain, shift, w_up, w_down, bias):
    hidden, pull = jax.vjp(layer_norm, x, gain, shift)
    hidden_low = hidden.astype(jnp.bfloat16)
    up_proj = product(hidden_low, w_up)
    act_low = jax.nn.silu(up_proj).astype(jnp.bfloat16)
    down_proj = cross_cols(act_low, w_down)
    return (x + 0.5 * (down_proj + bias), (pull, hidden_low, up_proj, act_low))


def feed_back(grad, kept, w_up, w_down):
    pull, hidden_low, up_proj, act_low = kept
    d_down = (0.5 * grad).astype(jnp.bfloat16)
    g_down = cross_rows(d_down, act_low)
    d_act = product(d_down, w_down)
    d_up = (d_act * silu_slope(up_proj)).astype(jnp.bfloat16)
    g_up = cross_rows(hidden_low, d_up)
    d_hidden = cross_cols(d_up, w_up)
    d_x, g_gain, g_shift = pull(d_hidden)
    return (grad + d_x, g_gain, g_shift, 0.5 * jnp.sum(grad, 0), g_up, g_down)


def scores_of(q_con, q_pos, key_low, pos_low, valid):
    content = jnp.einsum(
        "thd,shd->hts", split_heads(q_con), split_heads(key_low), preferred_element_type=jnp.float32
    )
    full = jnp.einsum(
        "thd,rhd->htr", split_heads(q_pos), split_heads(pos_low), preferred_element_type=jnp.float32
    )
    scores = (content + shift_rel(full)) * HEAD_DIM ** (-0.5)
    return jnp.where(valid[None, None, :], scores, -1e30)


def attention(x, vec, w_query, w_key, w_value, w_out, w_pos, table_low, valid):
    hidden, pull = jax.vjp(layer_norm, x, vec[2], vec[3])
    hidden_low = hidden.astype(jnp.bfloat16)
    query = product(hidden_low, w_query)
    key_low = product(hidden_low, w_key).astype(jnp.bfloat16)
    value_low = product(hidden_low, w_value).astype(jnp.bfloat16)
    pos_low = product(table_low, w_pos).astype(jnp.bfloat16)
    q_con = (query + vec[12]).astype(jnp.bfloat16)
    q_pos = (query + vec[13]).astype(jnp.bfloat16)
    scores = scores_of(q_con, q_pos, key_low, pos_low, valid)
    top = jnp.max(scores, -1, keepdims=True)
    expo = jnp.exp(scores - top)
    total = jnp.sum(expo, -1, keepdims=True)
    probs_low = (expo / total).astype(jnp.bfloat16)
    mixed = jnp.einsum(
        "hts,shd->thd", probs_low, split_heads(value_low), preferred_element_type=jnp.float32
    )
    mixed_low = mixed.reshape(x.shape[0], -1).astype(jnp.bfloat16)
    result = x + product(mixed_low, w_out) + vec[16]
    return (
        result,
        (pull, hidden_low, q_con, q_pos, key_low, value_low, pos_low, top, total, mixed_low),
    )


def attention_back(grad, kept, w_query, w_key, w_value, w_out, table_low, valid):
    pull, hidden_low, q_con, q_pos, key_low, value_low, pos_low, top, total, mixed_low = kept
    rows = grad.shape[0]
    d_out = grad.astype(jnp.bfloat16)
    g_out = cross_rows(mixed_low, d_out)
    d_mixed = split_heads(cross_cols(d_out, w_out).astype(jnp.bfloat16))
    scores = scores_of(q_con, q_pos, key_low, pos_low, valid)
    probs = jnp.exp(scores - top) / total
    probs_low = probs.astype(jnp.bfloat16)
    d_value = jnp.einsum(
        "hts,thd->shd", probs_low, d_mixed, preferred_element_type=jnp.float32
    ).reshape(rows, -1)
    d_probs = jnp.einsum(
        "thd,shd->hts", d_mixed, split_heads(value_low), preferred_element_type=jnp.float32
    )
    d_scores = probs * (d_probs - jnp.sum(probs * d_probs, -1, keepdims=True))
    d_scores = d_scores.astype(jnp.bfloat16) * HEAD_DIM ** (-0.5)
    d_con = jnp.einsum(
        "hts,shd->thd", d_scores, split_heads(key_low), preferred_element_type=jnp.float32
    ).reshape(rows, -1)
    d_key = jnp.einsum(
        "hts,thd->shd", d_scores, split_heads(q_con), preferred_element_type=jnp.float32
    ).reshape(rows, -1)
    d_full = unshift_rel(d_scores)
    d_qpos = jnp.einsum(
        "htr,rhd->thd", d_full, split_heads(pos_low), preferred_element_type=jnp.float32
    ).reshape(rows, -1)
    d_pos = jnp.einsum(
        "htr,thd->rhd", d_full, split_heads(q_pos), preferred_element_type=jnp.float32
    )
    d_pos = d_pos.reshape(2 * rows, -1).astype(jnp.bfloat16)
    g_pos = cross_rows(table_low, d_pos)
    d_query = (d_con + d_qpos).astype(jnp.bfloat16)
    d_key_low = d_key.astype(jnp.bfloat16)
    d_value_low = d_value.astype(jnp.bfloat16)
    g_query = cross_rows(hidden_low, d_query)
    g_key = cross_rows(hidden_low, d_key_low)
    g_value = cross_rows(hidden_low, d_value_low)
    d_hidden = (
        cross_cols(d_query, w_query)
        + cross_cols(d_key_low, w_key)
        + cross_cols(d_value_low, w_value)
    )
    d_x, g_gain, g_shift = pull(d_hidden)
    return (
        grad + d_x,
        g_gain,
        g_shift,
        jnp.sum(d_con, 0),
        jnp.sum(d_qpos, 0),
        jnp.sum(grad, 0),
        g_query,
        g_key,
        g_value,
        g_out,
        g_pos,
    )


def convolution(x, vec, w_value, w_gate, w_conv, mask, count):
    hidden, pull = jax.vjp(layer_norm, x, vec[4], vec[5])
    hidden_low = hidden.astype(jnp.bfloat16)
    gate_value = product(hidden_low, w_value)
    gate_sig = jax.nn.sigmoid(product(hidden_low, w_gate))
    glu = gate_value * gate_sig * mask
    conv, conv_pull = jax.vjp(depthwise, glu, vec[17:])
    summed = lax.psum(jnp.sum(conv * mask, 0), ("dp", "group"))
    middle = summed / count
    centred = conv - middle
    squared = lax.psum(jnp.sum(centred * centred * mask, 0), ("dp", "group"))
    spread = squared / count
    inverse = lax.rsqrt(spread + norm_epsilon)
    normal = centred * inverse
    normed = normal * vec[10] + vec[11]
    act_low = jax.nn.silu(normed).astype(jnp.bfloat16)
    result = x + product(act_low, w_conv)
    return (
        result,
        (pull, hidden_low, gate_value, gate_sig, conv_pull, normal, inverse, normed, act_low),
    )


def convolution_back(grad, kept, vec, w_value, w_gate, w_conv, mask, count):
    pull, hidden_low, gate_value, gate_sig, conv_pull, normal, inverse, normed, act_low = kept
    d_out = grad.astype(jnp.bfloat16)
    g_conv = cross_rows(act_low, d_out)
    d_normed = cross_cols(d_out, w_conv) * silu_slope(normed)
    local_shift = jnp.sum(d_normed, 0)
    local_gain = jnp.sum(d_normed * normal, 0)
    all_shift, all_gain = lax.psum((local_shift, local_gain), ("dp", "group"))
    d_conv = inverse * (
        d_normed * vec[10] - mask * (vec[10] * all_shift + normal * vec[10] * all_gain) / count
    )
    d_glu, g_kernel = conv_pull(d_conv)
    d_glu = d_glu * mask
    d_value = (d_glu * gate_sig).astype(jnp.bfloat16)
    d_gate = (d_glu * gate_value * gate_sig * (1.0 - gate_sig)).astype(jnp.bfloat16)
    g_value = cross_rows(hidden_low, d_value)
    g_gate = cross_rows(hidden_low, d_gate)
    d_hidden = cross_cols(d_value, w_value) + cross_cols(d_gate, w_gate)
    d_x, g_gain, g_shift = pull(d_hidden)
    return (grad + d_x, g_gain, g_shift, local_gain, local_shift, g_kernel, g_value, g_gate, g_conv)


def newton_schulz(mats):
    norms = jnp.sqrt(jnp.sum(mats * mats, axis=(1, 2), keepdims=True))
    current = mats / (norms + 1e-07)
    for sweep in range(NS_ITERS):
        low_x = current.astype(jnp.bfloat16)
        gram = jnp.einsum("nij,nkj->nik", low_x, low_x, preferred_element_type=jnp.float32)
        low_gram = gram.astype(jnp.bfloat16)
        poly = quintic_second * gram + quintic_third * jnp.einsum(
            "nij,njk->nik", low_gram, low_gram, preferred_element_type=jnp.float32
        )
        current = quintic_first * current + jnp.einsum(
            "nij,njk->nik", poly.astype(jnp.bfloat16), low_x, preferred_element_type=jnp.float32
        )
    return current


def muon(moment, grad, weight_low):
    weight = weight_low.astype(jnp.float32)
    moment_new = momentum_decay * moment + grad
    looked = grad + momentum_decay * moment_new
    ortho = newton_schulz(looked)
    scale = 0.2 * math.sqrt(max(weight.shape[1], weight.shape[2]))
    return (moment_new, weight * (1.0 - muon_rate * weight_decay) - muon_rate * scale * ortho)


def per_device(
    inputs,
    cotangent,
    lengths,
    square_slots,
    wide_slots,
    square_weights,
    wide_weights,
    vectors,
    square_moment,
    wide_moment,
    vector_moment,
    vector_second,
):
    groups = lax.axis_size("group")
    me = lax.axis_index("dp") * groups + lax.axis_index("group")
    length = lax.dynamic_index_in_dim(lengths, me, keepdims=False)
    count = jnp.sum(lengths).astype(jnp.float32)
    rows = inputs.shape[1]
    valid = jnp.arange(rows) < length
    mask = valid.astype(jnp.float32)[:, None]
    all_square, all_wide = (
        lax.all_gather(square_weights, "group", axis=0, tiled=True),
        lax.all_gather(wide_weights, "group", axis=0, tiled=True),
    )
    all_vector = lax.all_gather(vectors.astype(jnp.bfloat16), "group", axis=1, tiled=True).astype(
        vectors.dtype
    )
    table_low = rel_table(rows, D).astype(jnp.bfloat16)
    x = inputs[0].astype(jnp.float32)
    saved = []
    for depth in range(LAYERS):
        mats = [all_square[square_slots[8 * depth + role]] for role in range(8)]
        wides = [all_wide[wide_slots[4 * depth + role]] for role in range(4)]
        vec = all_vector[depth]
        x, first_kept = feed_forward(x, vec[0], vec[1], wides[0], wides[1], vec[14])
        x, attend_kept = attention(
            x, vec, mats[0], mats[1], mats[2], mats[3], mats[4], table_low, valid
        )
        x, conv_kept = convolution(x, vec, mats[5], mats[6], mats[7], mask, count)
        x, second_kept = feed_forward(x, vec[6], vec[7], wides[2], wides[3], vec[15])
        x, final_pull = jax.vjp(partial(masked_norm, mask=mask), x, vec[8], vec[9])
        saved.append(
            (mats, wides, vec, first_kept, attend_kept, conv_kept, second_kept, final_pull)
        )
    block_output = x.astype(jnp.bfloat16)[None]
    grad = cotangent[0].astype(jnp.float32)
    square_list = [None] * SQUARES
    wide_list = [None] * WIDES
    vector_list = [None] * LAYERS
    for depth in reversed(range(LAYERS)):
        mats, wides, vec, first_kept, attend_kept, conv_kept, second_kept, final_pull = saved[depth]
        grad, out_gain, out_shift = final_pull(grad)
        grad, ff2_gain, ff2_shift, ff2_bias, up_two, down_two = feed_back(
            grad, second_kept, wides[2], wides[3]
        )
        (
            grad,
            conv_gain,
            conv_shift,
            bn_gain,
            bn_shift,
            g_kernel,
            g_glu_value,
            g_glu_gate,
            g_conv,
        ) = convolution_back(grad, conv_kept, vec, mats[5], mats[6], mats[7], mask, count)
        (
            grad,
            att_gain,
            att_shift,
            g_ubias,
            g_vbias,
            att_bias,
            g_query,
            g_key,
            g_value,
            g_out,
            g_pos,
        ) = attention_back(grad, attend_kept, mats[0], mats[1], mats[2], mats[3], table_low, valid)
        grad, ff1_gain, ff1_shift, ff1_bias, up_one, down_one = feed_back(
            grad, first_kept, wides[0], wides[1]
        )
        for role, item in enumerate(
            [g_query, g_key, g_value, g_out, g_pos, g_glu_value, g_glu_gate, g_conv]
        ):
            square_list[8 * depth + role] = item
        for role, item in enumerate([up_one, down_one, up_two, down_two]):
            wide_list[4 * depth + role] = item
        vector_rows = jnp.stack(
            [
                ff1_gain,
                ff1_shift,
                att_gain,
                att_shift,
                conv_gain,
                conv_shift,
                ff2_gain,
                ff2_shift,
                out_gain,
                out_shift,
                bn_gain,
                bn_shift,
                g_ubias,
                g_vbias,
                ff1_bias,
                ff2_bias,
                att_bias,
            ]
        )
        vector_list[depth] = jnp.concatenate([vector_rows, g_kernel], 0)
    input_grad = grad[None]
    square_grad = jnp.stack(square_list)[jnp.argsort(square_slots)]
    wide_grad = jnp.stack(wide_list)[jnp.argsort(wide_slots)]
    vector_grad = jnp.stack(vector_list)
    owned = (
        lax.psum_scatter(
            square_grad.astype(jnp.bfloat16), "group", scatter_dimension=0, tiled=True
        ).astype(jnp.float32),
        lax.psum_scatter(
            wide_grad.astype(jnp.bfloat16), "group", scatter_dimension=0, tiled=True
        ).astype(jnp.float32),
        lax.psum_scatter(
            vector_grad.astype(jnp.bfloat16), "group", scatter_dimension=1, tiled=True
        ).astype(jnp.float32),
    )
    own_square, own_wide, own_vector = lax.psum((owned[0], owned[1], owned[2]), "dp")
    square_moment_new, square_new = muon(square_moment, own_square, square_weights)
    wide_moment_new, wide_new = muon(wide_moment, own_wide, wide_weights)
    moment_new = adam_first * vector_moment + (1.0 - adam_first) * own_vector
    second_new = adam_second * vector_second + (1.0 - adam_second) * own_vector * own_vector
    first_hat = moment_new / (1.0 - adam_first**STEP)
    second_hat = second_new / (1.0 - adam_second**STEP)
    vector_new = vectors - adam_rate * first_hat / (jnp.sqrt(second_hat) + adam_epsilon)
    return (
        block_output,
        input_grad,
        square_moment_new,
        square_new,
        wide_moment_new,
        wide_new,
        moment_new,
        second_new,
        vector_new,
    )


def solution(mesh):
    placed = (
        P(("dp", "group"), None, None),
        P(("dp", "group"), None, None),
        P(),
        P(),
        P(),
        P("group", None, None),
        P("group", None, None),
        P(None, "group", None),
        P("group", None, None),
        P("group", None, None),
        P(None, "group", None),
        P(None, "group", None),
    )
    return jax.shard_map(
        per_device,
        mesh=mesh,
        in_specs=placed,
        out_specs=(
            P(("dp", "group"), None, None),
            P(("dp", "group"), None, None),
            P("group", None, None),
            P("group", None, None),
            P("group", None, None),
            P("group", None, None),
            P(None, "group", None),
            P(None, "group", None),
            P(None, "group", None),
        ),
        check_vma=False,
    )
```

profile of v0, /device:TPU:0, one launch (start us, length us, event | category | flops | bytes accessed | tf_op | source)
XLA Modules:
  0.0 1706.2 jit_solution(11125722045578349605)
XLA Ops:
  43.5 7.0 all_gather.9
  78.2 100.5 %all-gather.3.cloned.1.call-done = bf16[8,512,2048]{2,1,0:T(8,128)(2,1)} async-done(((bf16[2,512,2048]{2,1,0:T(8,128)(2,1)}), bf16[8,512,2048]{2,1,0:T(8,128)(2,1)}) %all-gather.3.cloned.1.call-update) | async-done | bytes 16777232 | tf_op jit(solution)/shard_map/all_gather | solution.py:310
  197.2 8.0 reshape.1218
  222.4 39.4 %psum.77 = f32[512]{0:T(512)S(1)} all-reduce(f32[512]{0:T(512)S(1)} %get-tuple-element.170), channel_id=1, replica_groups=mesh['dp'=8,'group'=4] {'dp','group'}, use_global_device_ids=true, to_apply=%region_9.10 | all-reduce | flops 512 | bytes 4096 | tf_op jit(solution)/shard_map/psum | solution.py:224
  262.0 41.0 %psum.78 = f32[512]{0:T(512)S(1)} all-reduce(f32[512]{0:T(512)S(1)} %multiply_reduce_fusion.93), channel_id=1, replica_groups=mesh['dp'=8,'group'=4] {'dp','group'}, use_global_device_ids=true, to_apply=%region_12.13 | all-reduce | flops 512 | bytes 4096 | tf_op jit(solution)/shard_map/psum | solution.py:227
  336.7 8.0 reshape.1225
  370.3 39.3 %psum.79 = f32[512]{0:T(512)} all-reduce(f32[512]{0:T(512)} %get-tuple-element.166), channel_id=1, replica_groups=mesh['dp'=8,'group'=4] {'dp','group'}, use_global_device_ids=true, to_apply=%region_26.27 | all-reduce | flops 512 | bytes 4096 | tf_op jit(solution)/shard_map/psum | solution.py:224
  412.1 41.5 %psum.80 = f32[512]{0:T(512)} all-reduce(f32[512]{0:T(512)} %multiply_reduce_fusion.86), channel_id=1, replica_groups=mesh['dp'=8,'group'=4] {'dp','group'}, use_global_device_ids=true, to_apply=%region_28.29 | all-reduce | flops 512 | bytes 4096 | tf_op jit(solution)/shard_map/psum | solution.py:227
  475.1 39.8 %all-reduce.132 = (f32[512]{0:T(512)}, f32[512]{0:T(512)}) all-reduce(f32[512]{0:T(512)} %copy-done.291, f32[512]{0:T(512)S(1)} %get-tuple-element.116), channel_id=1, replica_groups=mesh['dp'=8,'group'=4] {'dp','group'}, use_global_device_ids=true, to_apply=%region_40.41 | all-reduce | flops 1024 | bytes 8192 | tf_op jit(solution)/shard_map/psum | solution.py:247
  515.7 6.8 multiply_reduce_fusion.33
  549.3 5.0 convolution_convert_fusion.6
  554.3 5.0 convolution_bitcast_fusion.19
  564.3 5.5 reshape.1343
  569.8 5.1 reshape.1227
  607.1 41.7 %all-reduce.131 = (f32[512]{0:T(512)}, f32[512]{0:T(512)S(1)}) all-reduce(f32[512]{0:T(512)} %copy-done.293, f32[512]{0:T(512)} %copy-done.292), channel_id=1, replica_groups=mesh['dp'=8,'group'=4] {'dp','group'}, use_global_device_ids=true, to_apply=%region_55.56 | all-reduce | flops 1024 | bytes 8192 | tf_op jit(solution)/shard_map/psum | solution.py:247
  649.5 6.9 multiply_reduce_fusion.68
  656.4 7.6 multiply_reduce_fusion.69
  689.3 5.0 convolution_bitcast_fusion.18
  713.7 5.4 reshape.1345
  719.1 5.1 reshape.1230
  775.0 8.5 gather_fusion
  797.6 8.5 fusion.451
  806.1 8.2 gather_fusion.1
  814.3 8.2 gather_fusion.2
  822.5 14.1 maximum_convert_fusion
  840.3 21.3 %reduce-scatter.3.cloned.1.call-done = bf16[4,512,512]{2,1,0:T(8,128)(2,1)} async-done(((bf16[16,512,512]{2,1,0:T(8,128)(2,1)}), bf16[4,512,512]{2,1,0:T(8,128)(2,1)}) %reduce-scatter.3.cloned.1.call-update) | async-done | bytes 2097168 | tf_op jit(solution)/shard_map/reduce_scatter | solution.py:403
  861.6 128.6 %reduce-scatter.5.cloned.1.call-done = bf16[2,512,2048]{2,1,0:T(8,128)(2,1)} async-done(((bf16[8,512,2048]{2,1,0:T(8,128)(2,1)}), bf16[2,512,2048]{2,1,0:T(8,128)(2,1)}) %reduce-scatter.5.cloned.1.call-update) | async-done | bytes 4194320 | tf_op jit(solution)/shard_map/reduce_scatter | solution.py:406
  990.2 487.6 %all-reduce.138 = (f32[4,512,512]{2,1,0:T(8,128)}, f32[2,512,2048]{2,1,0:T(8,128)}, f32[2,12,512]{2,0,1:T(2,128)S(1)}) all-reduce(bf16[4,512,512]{2,1,0:T(8,128)(2,1)} %reduce-scatter.3.cloned.1.call-done, bf16[2,512,2048]{2,1,0:T(8,128)(2,1)} %reduce-scatter.5.cloned.1.call-done, ...), channel_id=1, replica_groups=mesh['dp'=8,'group'=4] {'dp'}, use_global_device_ids=true, to_apply=%region_65.66 | all-reduce | flops 3158016 | bytes 18972672 | tf_op jit(solution)/shard_map/psum | solution.py:413
  1488.1 14.5 multiply_add_fusion.9
  1502.6 6.8 fusion.186
  1509.3 11.8 multiply_add_fusion.8
  1521.2 6.8 fusion.183
  1527.9 11.6 multiply_add_fusion.7
  1539.5 7.0 fusion.180
  1546.5 11.8 multiply_add_fusion.6
  1558.3 6.8 fusion.177
  1565.1 12.0 multiply_subtract_fusion.1
  1577.2 9.4 multiply_reduce_fusion
  1586.6 13.3 fusion.57
  1599.9 19.3 %multiply_add_fusion.3 = f32[2,512,2048]{2,1,0:T(8,128)} fusion(f32[2,512,512]{2,1,0:T(8,128)} %fusion.57, f32[2]{0:T(128)S(1)} %sqrt_add_fusion, f32[2,512,2048]{2,1,0:T(8,128)} %get-tuple-element.124, f32[2,512,2048]{2,1,0:T(8,128)} %get-tuple-element.130), kind=kOutput, calls=%fused_computation.12 | convolution fusion | flops 2705850368 | bytes 27262984 | tf_op jit(solution)/shard_map/nij,njk->nik/dot_general | solution.py:272
  1619.1 8.1 fusion.54
  1627.3 9.9 multiply_add_fusion.2
  1637.2 8.1 fusion.51
  1645.3 9.9 multiply_add_fusion.1
  1655.2 8.1 fusion.48
  1663.3 10.1 multiply_add_fusion
  1673.5 9.5 fusion.45
  1683.0 15.5 multiply_subtract_fusion
  (1002 shorter events, 321.9 us)
Async XLA Ops:
  7.2 67.1 %all-gather.5.cloned.1.call-start = ((), (), s32[]{:S(2)}) async-start(), calls=%async_computation.3 | async-start | bytes 10485760 | tf_op jit(solution)/shard_map/all_gather | solution.py:309
  7.9 32.4 %copy-start.347 = (s32[32]{0:T(128)S(1)}, s32[32]{0:T(128)}, u32[]{:S(2)}) copy-start(s32[32]{0:T(128)} %param.14) | copy-start | bytes 388
  7.9 35.5 %copy-start.106 = (f32[2,12,512]{2,0,1:T(2,128)S(1)}, f32[2,12,512]{2,0,1:T(2,128)}, u32[]{:S(2)}) copy-start(f32[2,12,512]{2,0,1:T(2,128)} %param.19) | copy-start | bytes 147460
  8.0 170.7 %all-gather.3.cloned.1.call-start = ((), (), s32[]{:S(2)}) async-start(), calls=%async_computation.2 | async-start | bytes 20971520 | tf_op jit(solution)/shard_map/all_gather | solution.py:310
  8.7 62.4 %copy-start.2 = (bf16[1,256,512]{2,1,0:T(8,128)(2,1)S(1)}, bf16[1,256,512]{2,1,0:T(8,128)(2,1)}, u32[]{:S(2)}) copy-start(bf16[1,256,512]{2,1,0:T(8,128)(2,1)} %param.12) | copy-start | bytes 786436
  8.7 830.9 %all-reduce.137.cloned.1.call-start = ((), (), s32[]{:S(2)}) async-start(), calls=%async_computation.6 | async-start | bytes 196608
  53.5 127.5 %copy-start = (bf16[512,512]{0,1:T(8,128)(2,1)}, bf16[512,512]{0,1:T(8,128)(2,1)S(1)}, u32[]{:S(2)}) copy-start(bf16[512,512]{0,1:T(8,128)(2,1)S(1)} %convert_element_type.450) | copy-start | bytes 1572868
  71.3 109.8 %copy-start.113 = (f32[256]{0:T(256)}, f32[256]{0:T(256)S(1)}, u32[]{:S(2)}) copy-start(f32[256]{0:T(256)S(1)} %broadcast_multiply_fusion.71) | copy-start | bytes 3076
  71.5 109.5 %copy-start.121 = (f32[256]{0:T(256)}, f32[256]{0:T(256)S(1)}, u32[]{:S(2)}) copy-start(f32[256]{0:T(256)S(1)} %fusion.387) | copy-start | bytes 3076
  72.2 232.6 %copy-start.136 = (f32[1,1,512]{2,0,1:T(1,128)}, f32[1,1,512]{2,0,1:T(1,128)S(1)}, u32[]{:S(2)}) copy-start(f32[1,1,512]{2,0,1:T(1,128)S(1)} %get-tuple-element.302) | copy-start | bytes 6148
  72.2 239.4 %copy-start.134 = (f32[1,1,512]{2,0,1:T(1,128)}, f32[1,1,512]{2,0,1:T(1,128)S(1)}, u32[]{:S(2)}) copy-start(f32[1,1,512]{2,0,1:T(1,128)S(1)} %get-tuple-element.297) | copy-start | bytes 6148
  72.2 147.9 %copy-start.140 = (f32[1,1,512]{2,0,1:T(1,128)}, f32[1,1,512]{2,0,1:T(1,128)S(1)}, u32[]{:S(2)}) copy-start(f32[1,1,512]{2,0,1:T(1,128)S(1)} %get-tuple-element.326) | copy-start | bytes 6148
  73.5 107.5 %copy-start.109 = (f32[1,1,512]{2,0,1:T(1,128)}, f32[1,1,512]{2,0,1:T(1,128)S(1)}, u32[]{:S(2)}) copy-start(f32[1,1,512]{2,0,1:T(1,128)S(1)} %get-tuple-element.344) | copy-start | bytes 6148
  73.5 107.5 %copy-start.132 = (f32[1,1,512]{2,0,1:T(1,128)}, f32[1,1,512]{2,0,1:T(1,128)S(1)}, u32[]{:S(2)}) copy-start(f32[1,1,512]{2,0,1:T(1,128)S(1)} %get-tuple-element.345) | copy-start | bytes 6148
  73.5 111.0 %copy-start.119 = (f32[1,1,512]{2,0,1:T(1,128)}, f32[1,1,512]{2,0,1:T(1,128)S(1)}, u32[]{:S(2)}) copy-start(f32[1,1,512]{2,0,1:T(1,128)S(1)} %get-tuple-element.342) | copy-start | bytes 6148
  73.6 146.6 %copy-start.142 = (f32[1,1,512]{2,0,1:T(1,128)}, f32[1,1,512]{2,0,1:T(1,128)S(1)}, u32[]{:S(2)}) copy-start(f32[1,1,512]{2,0,1:T(1,128)S(1)} %get-tuple-element.337) | copy-start | bytes 6148
  74.2 381.9 %copy-start.138 = (f32[1,1,512]{2,0,1:T(1,128)}, f32[1,1,512]{2,0,1:T(1,128)S(1)}, u32[]{:S(2)}) copy-start(f32[1,1,512]{2,0,1:T(1,128)S(1)} %get-tuple-element.254) | copy-start | bytes 6148
  74.2 396.1 %copy-start.115 = (f32[1,1,512]{2,0,1:T(1,128)}, f32[1,1,512]{2,0,1:T(1,128)S(1)}, u32[]{:S(2)}) copy-start(f32[1,1,512]{2,0,1:T(1,128)S(1)} %get-tuple-element.253) | copy-start | bytes 6148
  78.2 112.6 %copy-start.25 = (bf16[512,512]{0,1:T(8,128)(2,1)}, bf16[512,512]{0,1:T(8,128)(2,1)S(1)}, u32[]{:S(2)}) copy-start(bf16[512,512]{0,1:T(8,128)(2,1)S(1)} %convolution_convert_fusion.1) | copy-start | bytes 1572868
  186.7 22.1 %copy-start.78 = (bf16[256,512]{0,1:T(8,128)(2,1)}, bf16[256,512]{0,1:T(8,128)(2,1)S(1)}, u32[]{:S(2)}) copy-start(bf16[256,512]{0,1:T(8,128)(2,1)S(1)} %copy.102) | copy-start | bytes 786436
  188.3 24.8 %copy-start.80 = (bf16[256,512]{0,1:T(8,128)(2,1)}, bf16[256,512]{0,1:T(8,128)(2,1)S(1)}, u32[]{:S(2)}) copy-start(bf16[256,512]{0,1:T(8,128)(2,1)S(1)} %copy.100) | copy-start | bytes 786436
  217.8 85.2 %copy-start.16 = (f32[256,512]{1,0:T(8,128)}, f32[256,512]{1,0:T(8,128)S(1)}, u32[]{:S(2)}) copy-start(f32[256,512]{1,0:T(8,128)S(1)} %fusion.163) | copy-start | bytes 1572868
  220.1 84.4 %copy-start.4 = (f32[256,512]{1,0:T(8,128)}, f32[256,512]{1,0:T(8,128)S(1)}, u32[]{:S(2)}) copy-start(f32[256,512]{1,0:T(8,128)S(1)} %get-tuple-element.378) | copy-start | bytes 1572868
  222.4 82.1 %copy-start.20 = (f32[256,512]{1,0:T(8,128)}, f32[256,512]{1,0:T(8,128)S(1)}, u32[]{:S(2)}) copy-start(f32[256,512]{1,0:T(8,128)S(1)} %get-tuple-element.171) | copy-start | bytes 1572868
  261.8 42.7 %copy-start.212 = (f32[512]{0:T(512)}, f32[512]{0:T(512)S(1)}, u32[]{:S(2)}) copy-start(f32[512]{0:T(512)S(1)} %broadcast_divide_fusion.5) | copy-start | bytes 6148
  304.5 297.3 %copy-start.126 = (f32[256]{0:T(256)}, f32[256]{0:T(256)S(1)}, u32[]{:S(2)}) copy-start(f32[256]{0:T(256)S(1)} %broadcast_multiply_fusion.68) | copy-start | bytes 3076
  311.3 282.4 %copy-start.128 = (f32[256]{0:T(256)}, f32[256]{0:T(256)S(1)}, u32[]{:S(2)}) copy-start(f32[256]{0:T(256)S(1)} %broadcast_multiply_fusion.66) | copy-start | bytes 3076
  410.3 45.6 %copy-start.215 = (f32[512]{0:T(512)}, f32[512]{0:T(512)S(1)}, u32[]{:S(2)}) copy-start(f32[512]{0:T(512)S(1)} %broadcast_divide_fusion.4) | copy-start | bytes 6148
  454.2 17.2 %copy-start.310 = (f32[512]{0:T(512)}, f32[512]{0:T(512)S(1)}, u32[]{:S(2)}) copy-start(f32[512]{0:T(512)S(1)} %add_rsqrt_fusion) | copy-start | bytes 6148
  471.4 43.5 %copy-start.221 = (f32[1,1,512]{2,0,1:T(1,128)S(1)}, f32[1,1,512]{2,0,1:T(1,128)}, u32[]{:S(2)}) copy-start(f32[1,1,512]{2,0,1:T(1,128)} %get-tuple-element.256) | copy-start | bytes 6148
  605.4 58.7 %copy-start.141 = (f32[1,1,512]{2,0,1:T(1,128)S(1)}, f32[1,1,512]{2,0,1:T(1,128)}, u32[]{:S(2)}) copy-start(f32[1,1,512]{2,0,1:T(1,128)} %copy-done.140) | copy-start | bytes 6148
  605.4 58.7 %copy-start.145 = (f32[1,1,512]{2,0,1:T(1,128)S(1)}, f32[1,1,512]{2,0,1:T(1,128)}, u32[]{:S(2)}) copy-start(f32[1,1,512]{2,0,1:T(1,128)} %get-tuple-element.328) | copy-start | bytes 6148
  605.4 58.7 %copy-start.147 = (f32[1,1,512]{2,0,1:T(1,128)S(1)}, f32[1,1,512]{2,0,1:T(1,128)}, u32[]{:S(2)}) copy-start(f32[1,1,512]{2,0,1:T(1,128)} %get-tuple-element.329) | copy-start | bytes 6148
  605.4 58.7 %copy-start.149 = (f32[1,1,512]{2,0,1:T(1,128)S(1)}, f32[1,1,512]{2,0,1:T(1,128)}, u32[]{:S(2)}) copy-start(f32[1,1,512]{2,0,1:T(1,128)} %get-tuple-element.330) | copy-start | bytes 6148
  605.4 58.7 %copy-start.151 = (f32[1,1,512]{2,0,1:T(1,128)S(1)}, f32[1,1,512]{2,0,1:T(1,128)}, u32[]{:S(2)}) copy-start(f32[1,1,512]{2,0,1:T(1,128)} %get-tuple-element.331) | copy-start | bytes 6148
  605.4 58.7 %copy-start.153 = (f32[1,1,512]{2,0,1:T(1,128)S(1)}, f32[1,1,512]{2,0,1:T(1,128)}, u32[]{:S(2)}) copy-start(f32[1,1,512]{2,0,1:T(1,128)} %get-tuple-element.332) | copy-start | bytes 6148
  605.4 58.7 %copy-start.155 = (f32[1,1,512]{2,0,1:T(1,128)S(1)}, f32[1,1,512]{2,0,1:T(1,128)}, u32[]{:S(2)}) copy-start(f32[1,1,512]{2,0,1:T(1,128)} %get-tuple-element.333) | copy-start | bytes 6148
  605.4 58.7 %copy-start.157 = (f32[1,1,512]{2,0,1:T(1,128)S(1)}, f32[1,1,512]{2,0,1:T(1,128)}, u32[]{:S(2)}) copy-start(f32[1,1,512]{2,0,1:T(1,128)} %get-tuple-element.334) | copy-start | bytes 6148
  605.4 58.7 %copy-start.159 = (f32[1,1,512]{2,0,1:T(1,128)S(1)}, f32[1,1,512]{2,0,1:T(1,128)}, u32[]{:S(2)}) copy-start(f32[1,1,512]{2,0,1:T(1,128)} %get-tuple-element.335) | copy-start | bytes 6148
  605.4 58.7 %copy-start.161 = (f32[1,1,512]{2,0,1:T(1,128)S(1)}, f32[1,1,512]{2,0,1:T(1,128)}, u32[]{:S(2)}) copy-start(f32[1,1,512]{2,0,1:T(1,128)} %get-tuple-element.336) | copy-start | bytes 6148
  689.3 15.9 copy-start.345
  689.3 16.4 copy-start.331
  689.3 17.0 copy-start.330
  755.1 106.4 %reduce-scatter.3.cloned.1.call-start = ((), (), s32[]{:S(2)}) async-start(), calls=%async_computation.4 | async-start | bytes 10485760 | tf_op jit(solution)/shard_map/reduce_scatter | solution.py:403
  783.5 206.7 %reduce-scatter.5.cloned.1.call-start = ((), (), s32[]{:S(2)}) async-start(), calls=%async_computation.5 | async-start | bytes 20971520 | tf_op jit(solution)/shard_map/reduce_scatter | solution.py:406
  1683.0 15.5 copy-start.107
  1683.0 15.5 copy-start.111
  1683.0 15.5 copy-start.112
  (307 other events, 1190.5 us)
Sparse Core Ops, SparseCore 0:
  9.6 61.5 all-gather.4
  72.7 105.8 all-gather.2
  755.3 31.3 all-reduce.136
  789.8 71.7 reduce-scatter.2
  864.0 126.1 reduce-scatter.4
where the time goes:
time: 1720 us; the launch traced here: 1710 us
  blocking collectives  737 us (43%)
  matrix products  389 us (23%)
  waiting for transfers between devices  252 us (15%)
  local copies, waits for them, and re-layouts  161 us (9%)
  other arithmetic  101 us (6%)
  between operations  65.5 us (4%)
    psum x1, blocking collectives, per_device(): lax.psum((owned[0], owned[1], owned[2]), 'dp')  488 us
    reduce_scatter x1, waiting for transfers between devices, per_device(): lax.psum_scatter(wide_grad.astype(jnp.bfloat16), 'group', scatter_dimensi...  129 us
    dot_general x10, matrix products, newton_schulz(): jnp.einsum('nij,njk->nik', poly.astype(jnp.bfloat16), low_x, preferred_el...  126 us
    all_gather x1, waiting for transfers between devices, per_device(): lax.all_gather(wide_weights, 'group', axis=0, tiled=True)  100 us
    psum x2, blocking collectives, convolution(): squared = lax.psum(jnp.sum(centred * centred * mask, 0), ('dp', 'group'))  82.5 us
    psum x2, blocking collectives, convolution_back(): all_shift, all_gain = lax.psum((local_shift, local_gain), ('dp', 'group'))  81.6 us
    psum x2, blocking collectives, convolution(): summed = lax.psum(jnp.sum(conv * mask, 0), ('dp', 'group'))  78.7 us
    dot_general x10, matrix products, newton_schulz(): jnp.einsum('nij,nkj->nik', low_x, low_x, preferred_element_type=jnp.float32)  78 us
  transfers between devices with their start and end apart: 5, of which 3 were waited for; matrix products, arithmetic and copies ran while one was open for 5% of the time, Pallas kernels for 0%

commit v1 on v0

--- a/solution.py
+++ b/solution.py
@@ -4,6 +4,8 @@
 import jax
 import jax.numpy as jnp
 from jax import lax
+from jax.experimental import pallas as pl
+from jax.experimental.pallas import tpu as pltpu
 from jax.sharding import PartitionSpec as P
 
 D = 512
@@ -214,18 +216,103 @@
     )
 
 
-def convolution(x, vec, w_value, w_gate, w_conv, mask, count):
+def exchange_body(n_dp, n_group, reduce, x_ref, o_ref, first, second, send_one, recv_one, send_two, recv_two):
+    dp, group = lax.axis_index("dp"), lax.axis_index("group")
+    near = [{"dp": dp, "group": lax.rem(group + k, n_group)} for k in range(1, n_group)]
+    far = [{"dp": lax.rem(dp + k, n_dp), "group": group} for k in range(1, n_dp)]
+    barrier = pltpu.get_barrier_semaphore()
+    for peer in near + far:
+        pl.semaphore_signal(barrier, inc=1, device_id=peer, device_id_type=pl.DeviceIdType.MESH)
+    pl.semaphore_wait(barrier, n_group + n_dp - 2)
+    copies = []
+    for k, peer in enumerate(near):
+        copies.append(
+            pltpu.make_async_remote_copy(
+                src_ref=x_ref.at[peer["group"]] if reduce else x_ref.at[0],
+                dst_ref=first.at[group],
+                send_sem=send_one.at[k],
+                recv_sem=recv_one.at[k],
+                device_id=peer,
+                device_id_type=pl.DeviceIdType.MESH,
+            )
+        )
+        copies[-1].start()
+    first[group] = x_ref[group] if reduce else x_ref[0]
+    for copy in copies:
+        copy.wait()
+    if reduce:
+        total = first[0]
+        for k in range(1, n_group):
+            total = total + first[k]
+        second[dp] = total
+    else:
+        second[dp] = first[...]
+    copies = []
+    for k, peer in enumerate(far):
+        copies.append(
+            pltpu.make_async_remote_copy(
+                src_ref=second.at[dp],
+                dst_ref=second.at[dp],
+                send_sem=send_two.at[k],
+                recv_sem=recv_two.at[k],
+                device_id=peer,
+                device_id_type=pl.DeviceIdType.MESH,
+            )
+        )
+        copies[-1].start()
+    for copy in copies:
+        copy.wait()
+    if reduce:
+        total = second[0]
+        for k in range(1, n_dp):
+            total = total + second[k]
+        o_ref[...] = total
+    else:
+        o_ref[...] = second[...]
+
+
+def exchange(x, reduce, collective_id):
+    n_dp, n_group = lax.axis_size("dp"), lax.axis_size("group")
+    block = x.shape[1:]
+    held = (n_dp,) + block if reduce else (n_dp, n_group) + block
+    return pl.pallas_call(
+        partial(exchange_body, n_dp, n_group, reduce),
+        out_shape=jax.ShapeDtypeStruct(block if reduce else held, x.dtype),
+        in_specs=[pl.BlockSpec(memory_space=pltpu.VMEM)],
+        out_specs=pl.BlockSpec(memory_space=pltpu.VMEM),
+        scratch_shapes=[
+            pltpu.VMEM((n_group,) + block, x.dtype),
+            pltpu.VMEM(held, x.dtype),
+            pltpu.SemaphoreType.DMA((n_group - 1,)),
+            pltpu.SemaphoreType.DMA((n_group - 1,)),
+            pltpu.SemaphoreType.DMA((n_dp - 1,)),
+            pltpu.SemaphoreType.DMA((n_dp - 1,)),
+        ],
+        compiler_params=pltpu.CompilerParams(collective_id=collective_id, has_side_effects=True),
+    )(x)
+
+
+def gather_pairs(first, second):
+    width = first.shape[0]
+    block = jnp.stack([first, second]).reshape(1, 8, width // 4)
+    return exchange(block, False, 1).reshape(-1, 2, width)
+
+
+def convolution(x, vec, w_value, w_gate, w_conv, mask, count, lengths):
     hidden, pull = jax.vjp(layer_norm, x, vec[4], vec[5])
     hidden_low = hidden.astype(jnp.bfloat16)
     gate_value = product(hidden_low, w_value)
     gate_sig = jax.nn.sigmoid(product(hidden_low, w_gate))
     glu = gate_value * gate_sig * mask
     conv, conv_pull = jax.vjp(depthwise, glu, vec[17:])
-    summed = lax.psum(jnp.sum(conv * mask, 0), ("dp", "group"))
-    middle = summed / count
+    summed = jnp.sum(conv * mask, 0)
+    apart = (conv - summed / jnp.sum(mask)) * mask
+    pairs = gather_pairs(summed, jnp.sum(apart * apart, 0))
+    numbers = lengths.astype(jnp.float32)[:, None]
+    middle = jnp.sum(pairs[:, 0], 0) / count
+    between = pairs[:, 0] / numbers - middle
+    spread = jnp.sum(pairs[:, 1] + numbers * between * between, 0) / count
     centred = conv - middle
-    squared = lax.psum(jnp.sum(centred * centred * mask, 0), ("dp", "group"))
-    spread = squared / count
     inverse = lax.rsqrt(spread + norm_epsilon)
     normal = centred * inverse
     normed = normal * vec[10] + vec[11]
@@ -244,7 +331,8 @@
     d_normed = cross_cols(d_out, w_conv) * silu_slope(normed)
     local_shift = jnp.sum(d_normed, 0)
     local_gain = jnp.sum(d_normed * normal, 0)
-    all_shift, all_gain = lax.psum((local_shift, local_gain), ("dp", "group"))
+    pairs = gather_pairs(local_shift, local_gain)
+    all_shift, all_gain = jnp.sum(pairs[:, 0], 0), jnp.sum(pairs[:, 1], 0)
     d_conv = inverse * (
         d_normed * vec[10] - mask * (vec[10] * all_shift + normal * vec[10] * all_gain) / count
     )
@@ -259,29 +347,62 @@
     return (grad + d_x, g_gain, g_shift, local_gain, local_shift, g_kernel, g_value, g_gate, g_conv)
 
 
-def newton_schulz(mats):
-    norms = jnp.sqrt(jnp.sum(mats * mats, axis=(1, 2), keepdims=True))
-    current = mats / (norms + 1e-07)
-    for sweep in range(NS_ITERS):
-        low_x = current.astype(jnp.bfloat16)
-        gram = jnp.einsum("nij,nkj->nik", low_x, low_x, preferred_element_type=jnp.float32)
+def muon_body(scale, moment_ref, grad_ref, weight_ref, moment_out, weight_out, current, low):
+    tile = 512
+    parts = [pl.ds(k, tile) for k in range(0, current.shape[1], tile)]
+    total = jnp.zeros((1, 1), jnp.float32)
+    for part in parts:
+        grad = grad_ref[:, part].astype(jnp.float32)
+        moment_new = momentum_decay * moment_ref[0, :, part] + grad
+        moment_out[0, :, part] = moment_new
+        looked = grad + momentum_decay * moment_new
+        current[:, part] = looked
+        total = total + jnp.sum(looked * looked, keepdims=True)
+    factor = 1.0 / (jnp.sqrt(total) + 1e-07)
+    for part in parts:
+        current[:, part] = current[:, part] * factor
+
+    def sweep(_, carry):
+        gram = jnp.zeros((current.shape[0], current.shape[0]), jnp.float32)
+        for part in parts:
+            low[:, part] = current[:, part].astype(jnp.bfloat16)
+            gram = gram + cross_cols(low[:, part], low[:, part])
         low_gram = gram.astype(jnp.bfloat16)
-        poly = quintic_second * gram + quintic_third * jnp.einsum(
-            "nij,njk->nik", low_gram, low_gram, preferred_element_type=jnp.float32
-        )
-        current = quintic_first * current + jnp.einsum(
-            "nij,njk->nik", poly.astype(jnp.bfloat16), low_x, preferred_element_type=jnp.float32
-        )
-    return current
-
-
-def muon(moment, grad, weight_low):
-    weight = weight_low.astype(jnp.float32)
-    moment_new = momentum_decay * moment + grad
-    looked = grad + momentum_decay * moment_new
-    ortho = newton_schulz(looked)
-    scale = 0.2 * math.sqrt(max(weight.shape[1], weight.shape[2]))
-    return (moment_new, weight * (1.0 - muon_rate * weight_decay) - muon_rate * scale * ortho)
+        poly = quintic_second * gram + quintic_third * product(low_gram, low_gram)
+        poly = poly.astype(jnp.bfloat16)
+        for part in parts:
+            current[:, part] = quintic_first * current[:, part] + product(poly, low[:, part])
+        return carry
+
+    lax.fori_loop(0, NS_ITERS, sweep, 0)
+    for part in parts:
+        weight = weight_ref[0, :, part].astype(jnp.float32)
+        weight_out[0, :, part] = (
+            weight * (1.0 - muon_rate * weight_decay) - muon_rate * scale * current[:, part]
+        )
+
+
+def muon(moment, grads, weight_low, first):
+    many, rows, columns = moment.shape
+    scale = 0.2 * math.sqrt(max(rows, columns))
+    stack = pl.BlockSpec((1, rows, columns), lambda i: (i, 0, 0))
+    return pl.pallas_call(
+        partial(muon_body, scale),
+        grid=(many,),
+        out_shape=[jax.ShapeDtypeStruct(moment.shape, jnp.float32)] * 2,
+        in_specs=[stack, pl.BlockSpec((rows, columns), lambda i: (0, first + i)), stack],
+        out_specs=[stack, stack],
+        scratch_shapes=[
+            pltpu.VMEM((rows, columns), jnp.float32),
+            pltpu.VMEM((rows, columns), jnp.bfloat16),
+        ],
+        compiler_params=pltpu.CompilerParams(vmem_limit_bytes=56 * 1024 * 1024),
+    )(moment, grads, weight_low)
+
+
+def slot_order(slots):
+    places = jnp.arange(slots.shape[0])
+    return jnp.sum(jnp.where(slots[None, :] == places[:, None], places[None, :], 0), 1)
 
 
 def per_device(
@@ -323,7 +444,7 @@
         x, attend_kept = attention(
             x, vec, mats[0], mats[1], mats[2], mats[3], mats[4], table_low, valid
         )
-        x, conv_kept = convolution(x, vec, mats[5], mats[6], mats[7], mask, count)
+        x, conv_kept = convolution(x, vec, mats[5], mats[6], mats[7], mask, count, lengths)
         x, second_kept = feed_forward(x, vec[6], vec[7], wides[2], wides[3], vec[15])
         x, final_pull = jax.vjp(partial(masked_norm, mask=mask), x, vec[8], vec[9])
         saved.append(
@@ -331,8 +452,8 @@
         )
     block_output = x.astype(jnp.bfloat16)[None]
     grad = cotangent[0].astype(jnp.float32)
-    square_list = [None] * SQUARES
-    wide_list = [None] * WIDES
+    square_list = [None] * LAYERS
+    wide_list = [None] * LAYERS
     vector_list = [None] * LAYERS
     for depth in reversed(range(LAYERS)):
         mats, wides, vec, first_kept, attend_kept, conv_kept, second_kept, final_pull = saved[depth]
@@ -367,12 +488,13 @@
         grad, ff1_gain, ff1_shift, ff1_bias, up_one, down_one = feed_back(
             grad, first_kept, wides[0], wides[1]
         )
-        for role, item in enumerate(
-            [g_query, g_key, g_value, g_out, g_pos, g_glu_value, g_glu_gate, g_conv]
-        ):
-            square_list[8 * depth + role] = item
-        for role, item in enumerate([up_one, down_one, up_two, down_two]):
-            wide_list[4 * depth + role] = item
+        layer_grads = [g_query, g_key, g_value, g_out, g_pos, g_glu_value, g_glu_gate, g_conv]
+        layer_grads += [up_one, down_one, up_two, down_two]
+        merged = jnp.concatenate([item.astype(jnp.bfloat16) for item in layer_grads], 1)
+        merged = lax.psum_scatter(merged, "group", scatter_dimension=0, tiled=True)
+        merged = lax.psum_scatter(merged, "dp", scatter_dimension=0, tiled=True)
+        square_list[depth] = merged[:, : 8 * D].reshape(-1, 8, D)
+        wide_list[depth] = merged[:, 8 * D :].reshape(-1, 4, merged.shape[1] // 6)
         vector_rows = jnp.stack(
             [
                 ff1_gain,
@@ -396,23 +518,24 @@
         )
         vector_list[depth] = jnp.concatenate([vector_rows, g_kernel], 0)
     input_grad = grad[None]
-    square_grad = jnp.stack(square_list)[jnp.argsort(square_slots)]
-    wide_grad = jnp.stack(wide_list)[jnp.argsort(wide_slots)]
+    square_grad = jnp.concatenate(square_list, 1)[:, slot_order(square_slots)]
+    wide_grad = jnp.concatenate(wide_list, 1)[:, slot_order(wide_slots)]
+    pieces = square_grad.shape[0]
+    owned = jnp.concatenate(
+        [square_grad.reshape(pieces, groups, -1), wide_grad.reshape(pieces, groups, -1)], 2
+    )
+    owned = lax.all_to_all(owned, "group", split_axis=1, concat_axis=0)
+    owned = lax.all_gather(owned, "dp", axis=1)
+    owned = owned.reshape(D, -1)
+    square_moment_new, square_new = muon(square_moment, owned, square_weights, 0)
+    wide_moment_new, wide_new = muon(
+        wide_moment, owned, wide_weights, square_moment.shape[0] * D // wide_moment.shape[2]
+    )
     vector_grad = jnp.stack(vector_list)
-    owned = (
-        lax.psum_scatter(
-            square_grad.astype(jnp.bfloat16), "group", scatter_dimension=0, tiled=True
-        ).astype(jnp.float32),
-        lax.psum_scatter(
-            wide_grad.astype(jnp.bfloat16), "group", scatter_dimension=0, tiled=True
-        ).astype(jnp.float32),
-        lax.psum_scatter(
-            vector_grad.astype(jnp.bfloat16), "group", scatter_dimension=1, tiled=True
-        ).astype(jnp.float32),
-    )
-    own_square, own_wide, own_vector = lax.psum((owned[0], owned[1], owned[2]), "dp")
-    square_moment_new, square_new = muon(square_moment, own_square, square_weights)
-    wide_moment_new, wide_new = muon(wide_moment, own_wide, wide_weights)
+    layers, vector_rows, width = vectors.shape
+    vector_grad = vector_grad.reshape(layers, groups, vector_rows, width).swapaxes(0, 1)
+    own_vector = exchange(vector_grad.reshape(groups, layers * vector_rows, width), True, 2)
+    own_vector = own_vector.reshape(vectors.shape)
     moment_new = adam_first * vector_moment + (1.0 - adam_first) * own_vector
     second_new = adam_second * vector_second + (1.0 - adam_second) * own_vector * own_vector
     first_hat = moment_new / (1.0 - adam_first**STEP)

time: 1720 us -> 1140 us (0.66)
  blocking collectives: 737 us -> 22.1 us
  waiting for transfers between devices: 252 us -> 486 us
  matrix products: 389 us -> 193 us
  Pallas kernels: 0 us -> 136 us
  other arithmetic: 101 us -> 59.9 us
    psum x7 -> x0, blocking collectives: 730 us -> none  [the longest x1 488 us: per_device(): lax.psum((owned[0], owned[1], owned[2]), 'dp')]
    dot_general x20 -> x0, matrix products: 204 us -> none  [the longest x10 126 us: newton_schulz(): jnp.einsum('nij,njk->nik', poly.astype(jnp.bfloat16), low_x, preferred_el...]
    reduce_scatter x2 -> x4, waiting for transfers between devices: 150 us -> 312 us  [the longest x2 158 us: per_device(): merged = lax.psum_scatter(merged, 'group', scatter_dimension=0, tiled=True)]
    pallas_call x0 -> x7, Pallas kernels: none -> 136 us  [the longest x2 67.9 us: muon(): pl.pallas_call(partial(muon_body, scale), grid=(many,), out_shape=[jax.Sh...]
    all_gather x0 -> x1, waiting for transfers between devices: none -> 73.3 us  [per_device(): owned = lax.all_gather(owned, 'dp', axis=1)]
    gather x4, local copies, waits for them, and re-layouts: 33.5 us -> 1.59 us  [the longest x2 0.88 us: per_device(): wide_grad = jnp.concatenate(wide_list, 1)[:, slot_order(wide_slots)]]
    convert_element_type x0 -> x16, local copies, waits for them, and re-layouts: none -> 27.9 us  [per_device(): item.astype(jnp.bfloat16)]
    unnamed x707 -> x641, local copies, waits for them, and re-layouts: 41.3 us -> 50.2 us
  transfers between devices with their start and end apart: 5 -> 7, of which waited for: 3 -> 6; matrix products, arithmetic and copies ran while one was open for 5% -> 6% of each run, Pallas kernels for 0% -> 2%
where the time goes in v1:
time: 1140 us; the launch traced here: 1130 us
  waiting for transfers between devices  486 us (43%)
  matrix products  193 us (17%)
  local copies, waits for them, and re-layouts  165 us (14%)
  Pallas kernels  136 us (12%)
  between operations  65 us (6%)
  other arithmetic  59.9 us (5%)
  blocking collectives  22.1 us (2%)
    reduce_scatter x2, waiting for transfers between devices, per_device(): merged = lax.psum_scatter(merged, 'group', scatter_dimension=0, tiled=True)  158 us
    reduce_scatter x2, waiting for transfers between devices, per_device(): merged = lax.psum_scatter(merged, 'dp', scatter_dimension=0, tiled=True)  154 us
    all_gather x1, waiting for transfers between devices, per_device(): lax.all_gather(wide_weights, 'group', axis=0, tiled=True)  99.8 us
    all_gather x1, waiting for transfers between devices, per_device(): owned = lax.all_gather(owned, 'dp', axis=1)  73.3 us
    pallas_call x2, Pallas kernels, muon(): pl.pallas_call(partial(muon_body, scale), grid=(many,), out_shape=[jax.Sh...  67.9 us
    pallas_call x5, Pallas kernels, exchange(): pl.pallas_call(partial(exchange_body, n_dp, n_group, reduce), out_shape=j...  67.9 us
    dot_general x22, matrix products, cross_cols(): lax.dot_general(left, right, (((1,), (1,)), ((), ())), preferred_element_...  50.4 us
    unnamed x641, local copies, waits for them, and re-layouts  50.2 us
  transfers between devices with their start and end apart: 7, of which 6 were waited for; matrix products, arithmetic and copies ran while one was open for 6% of the time, Pallas kernels for 2%

profile of v1, /device:TPU:0, one launch (start us, length us, event | category | flops | bytes accessed | tf_op | source)
XLA Modules:
  0.0 1127.5 jit_solution(13137782425227555230)
XLA Ops:
  44.1 7.0 all_gather.12
  78.8 99.8 %all-gather.5.cloned.1.call-done = bf16[8,512,2048]{2,1,0:T(8,128)(2,1)} async-done(((bf16[2,512,2048]{2,1,0:T(8,128)(2,1)}), bf16[8,512,2048]{2,1,0:T(8,128)(2,1)}) %all-gather.5.cloned.1.call-update) | async-done | bytes 16777232 | tf_op jit(solution)/shard_map/all_gather | solution.py:431
  181.1 3.2 fusion.386
  192.9 3.2 slice.1011
  196.1 8.0 reshape.1318
  219.7 2.9 multiply_reduce_fusion.92
  224.1 11.3 %shard_map.187 = f32[8,4,8,128]{3,2,1,0:T(8,128)} custom-call(f32[1,8,128]{2,1,0:T(8,128)} %reshape.1319.x_ref), custom_call_target="tpu_custom_call" | custom-call | tf_op jit(solution)/shard_map/pallas_call | solution.py:278
  241.0 3.2 fusion.390
  247.7 3.2 fusion.391
  261.2 3.2 slice.1063
  264.4 19.7 %reshape.1327 = f32[8,256,511]{2,1,0:T(8,128)} reshape(f32[8,130816]{1,0:T(8,128)} %slice.1063) | data formatting | bytes 8372224 | tf_op jit(solution)/shard_map/reshape | solution.py:56
  284.1 3.0 slice.1064
  287.1 2.9 copy.314
  302.7 3.1 multiply_reduce_fusion.85
  307.3 12.4 %shard_map.188 = f32[8,4,8,128]{3,2,1,0:T(8,128)} custom-call(f32[1,8,128]{2,1,0:T(8,128)} %reshape.1328.x_ref), custom_call_target="tpu_custom_call" | custom-call | tf_op jit(solution)/shard_map/pallas_call | solution.py:278
  325.9 3.2 fusion.395
  331.3 2.9 fusion.12
  334.2 3.4 multiply_reduce_fusion.33
  341.8 11.5 %shard_map.189 = f32[8,4,8,128]{3,2,1,0:T(8,128)} custom-call(f32[1,8,128]{2,1,0:T(8,128)} %reshape.1330.x_ref), custom_call_target="tpu_custom_call" | custom-call | tf_op jit(solution)/shard_map/pallas_call | solution.py:278
  371.8 3.5 convolution_convert_fusion.29
  376.9 4.3 fusion.78
  381.1 3.7 convolution_convert_fusion.30
  384.9 3.8 convolution_bitcast_fusion.3
  392.4 4.8 reshape.1450
  397.2 5.1 reshape.1333
  415.8 3.5 multiply_reduce_fusion.36
  421.1 2.9 fusion.14
  424.1 3.4 multiply_reduce_fusion.69
  433.5 12.4 %shard_map.190 = f32[8,4,8,128]{3,2,1,0:T(8,128)} custom-call(f32[1,8,128]{2,1,0:T(8,128)} %reshape.1335.x_ref), custom_call_target="tpu_custom_call" | custom-call | tf_op jit(solution)/shard_map/pallas_call | solution.py:278
  447.7 5.7 multiply_reduce_fusion.66
  471.4 3.6 convolution_convert_fusion.26
  477.8 4.7 fusion.81
  482.6 4.9 convolution_convert_fusion.27
  487.5 5.0 convolution_bitcast_fusion.2
  509.0 5.0 reshape.1452
  514.0 5.1 reshape.1338
  559.5 3.0 fusion.6
  597.6 3.0 fusion.8
  607.6 56.6 %reduce-scatter.5.cloned.1.call-done = bf16[128,12288]{1,0:T(8,128)(2,1)} async-done(((bf16[512,12288]{1,0:T(8,128)(2,1)}), bf16[128,12288]{1,0:T(8,128)(2,1)}) %reduce-scatter.5.cloned.1.call-update) | async-done | bytes 3145744 | tf_op jit(solution)/shard_map/reduce_scatter | solution.py:494
  664.3 101.5 %reduce-scatter.9.cloned.1.call-done = bf16[128,12288]{1,0:T(8,128)(2,1)} async-done(((bf16[512,12288]{1,0:T(8,128)(2,1)}), bf16[128,12288]{1,0:T(8,128)(2,1)}) %reduce-scatter.9.cloned.1.call-update) | async-done | bytes 3145744 | tf_op jit(solution)/shard_map/reduce_scatter | solution.py:494
  766.1 77.5 %reduce-scatter.7.cloned.1.call-done = bf16[16,12288]{1,0:T(8,128)(2,1)} async-done(((bf16[128,12288]{1,0:T(8,128)(2,1)}), bf16[16,12288]{1,0:T(8,128)(2,1)}) %reduce-scatter.7.cloned.1.call-update) | async-done | bytes 393232 | tf_op jit(solution)/shard_map/reduce_scatter | solution.py:495
  844.5 76.1 %reduce-scatter.11.cloned.1.call-done = bf16[16,12288]{1,0:T(8,128)(2,1)} async-done(((bf16[128,12288]{1,0:T(8,128)(2,1)}), bf16[16,12288]{1,0:T(8,128)(2,1)}) %reduce-scatter.11.cloned.1.call-update) | async-done | bytes 393232 | tf_op jit(solution)/shard_map/reduce_scatter | solution.py:495
  925.3 15.1 %all_to_all.15 = bf16[1,16,4,6144]{3,1,0,2:T(8,128)(2,1)} all-to-all(bf16[1,16,4,6144]{3,1,0,2:T(8,128)(2,1)S(1)} %copy.291), channel_id=1, replica_groups=mesh['dp'=8,'group'=4] {'group'}, dimensions={2} | all-to-all | bytes 1572864 | tf_op jit(solution)/shard_map/all_to_all | solution.py:527
  948.7 20.2 %shard_map.193 = f32[24,512]{1,0:T(8,128)} custom-call(f32[4,24,512]{2,1,0:T(8,128)} %copy.296.x_ref), custom_call_target="tpu_custom_call" | custom-call | tf_op jit(solution)/shard_map/pallas_call | solution.py:278
  972.8 73.3 %all-gather.9.cloned.1.call-done = bf16[4,8,16,1,6144]{4,2,3,0,1:T(8,128)(2,1)} async-done(((bf16[4,1,16,1,6144]{4,2,3,0,1:T(8,128)(2,1)}), bf16[4,8,16,1,6144]{4,2,3,0,1:T(8,128)(2,1)}) %all-gather.9.cloned.1.call-update) | async-done | bytes 6291472 | tf_op jit(solution)/shard_map/all_gather | solution.py:528
  1046.2 6.2 copy.293
  1052.3 28.5 %shard_map.191 = (f32[4,512,512]{2,1,0:T(8,128)}, f32[4,512,512]{2,1,0:T(8,128)}) custom-call(f32[4,512,512]{2,1,0:T(8,128)} %moment_ref.2, bf16[512,6144]{1,0:T(8,128)(2,1)} %bitcast.687, bf16[4,512,512]{2,1,0:T(8,128)(2,1)} %weight_ref.2), custom_call_target="tpu_custom_call" | custom-call | tf_op jit(solution)/shard_map/pallas_call | solution.py:389
  1080.8 39.4 %shard_map.192 = (f32[2,512,2048]{2,1,0:T(8,128)}, f32[2,512,2048]{2,1,0:T(8,128)}) custom-call(f32[2,512,2048]{2,1,0:T(8,128)} %moment_ref.3, bf16[512,6144]{1,0:T(8,128)(2,1)} %bitcast.688, bf16[2,512,2048]{2,1,0:T(8,128)(2,1)} %weight_ref.3), custom_call_target="tpu_custom_call" | custom-call | tf_op jit(solution)/shard_map/pallas_call | solution.py:389
  (936 shorter events, 273.3 us)
Async XLA Ops:
  7.2 67.8 %all-gather.7.cloned.1.call-start = ((), (), s32[]{:S(2)}) async-start(), calls=%async_computation.6 | async-start | bytes 10485760 | tf_op jit(solution)/shard_map/all_gather | solution.py:430
  7.9 36.1 %copy-start.112 = (f32[2,12,512]{2,0,1:T(2,128)S(1)}, f32[2,12,512]{2,0,1:T(2,128)}, u32[]{:S(2)}) copy-start(f32[2,12,512]{2,0,1:T(2,128)} %param.19) | copy-start | bytes 147460
  8.0 170.7 %all-gather.5.cloned.1.call-start = ((), (), s32[]{:S(2)}) async-start(), calls=%async_computation.5 | async-start | bytes 20971520 | tf_op jit(solution)/shard_map/all_gather | solution.py:431
  8.7 62.4 %copy-start.28 = (bf16[1,256,512]{2,1,0:T(8,128)(2,1)S(1)}, bf16[1,256,512]{2,1,0:T(8,128)(2,1)}, u32[]{:S(2)}) copy-start(bf16[1,256,512]{2,1,0:T(8,128)(2,1)} %param.12) | copy-start | bytes 786436
  8.7 655.5 %reduce-scatter.5.cloned.1.call-start = ((), (), s32[]{:S(2)}) async-start(), calls=%async_computation.7 | async-start | bytes 15728640 | tf_op jit(solution)/shard_map/reduce_scatter | solution.py:494
  54.1 126.9 %copy-start.1 = (bf16[512,512]{0,1:T(8,128)(2,1)}, bf16[512,512]{0,1:T(8,128)(2,1)S(1)}, u32[]{:S(2)}) copy-start(bf16[512,512]{0,1:T(8,128)(2,1)S(1)} %convert_element_type.415) | copy-start | bytes 1572868
  71.3 109.7 %copy-start.134 = (f32[256]{0:T(256)}, f32[256]{0:T(256)S(1)}, u32[]{:S(2)}) copy-start(f32[256]{0:T(256)S(1)} %broadcast_multiply_fusion.75) | copy-start | bytes 3076
  71.5 109.5 %copy-start.208 = (f32[256]{0:T(256)}, f32[256]{0:T(256)S(1)}, u32[]{:S(2)}) copy-start(f32[256]{0:T(256)S(1)} %fusion.150) | copy-start | bytes 3076
  71.5 109.5 %copy-start.194 = (f32[256]{0:T(256)}, f32[256]{0:T(256)S(1)}, u32[]{:S(2)}) copy-start(f32[256]{0:T(256)S(1)} %fusion.329) | copy-start | bytes 3076
  72.2 146.8 %copy-start.144 = (f32[1,1,512]{2,0,1:T(1,128)}, f32[1,1,512]{2,0,1:T(1,128)S(1)}, u32[]{:S(2)}) copy-start(f32[1,1,512]{2,0,1:T(1,128)S(1)} %get-tuple-element.334) | copy-start | bytes 6148
  72.2 146.8 %copy-start.146 = (f32[1,1,512]{2,0,1:T(1,128)}, f32[1,1,512]{2,0,1:T(1,128)S(1)}, u32[]{:S(2)}) copy-start(f32[1,1,512]{2,0,1:T(1,128)S(1)} %get-tuple-element.335) | copy-start | bytes 6148
  72.2 166.3 %copy-start.142 = (f32[1,1,512]{2,0,1:T(1,128)}, f32[1,1,512]{2,0,1:T(1,128)S(1)}, u32[]{:S(2)}) copy-start(f32[1,1,512]{2,0,1:T(1,128)S(1)} %get-tuple-element.329) | copy-start | bytes 6148
  72.2 173.1 %copy-start.138 = (f32[1,1,512]{2,0,1:T(1,128)}, f32[1,1,512]{2,0,1:T(1,128)S(1)}, u32[]{:S(2)}) copy-start(f32[1,1,512]{2,0,1:T(1,128)S(1)} %get-tuple-element.324) | copy-start | bytes 6148
  72.2 226.6 %copy-start.122 = (f32[1,1,512]{2,0,1:T(1,128)}, f32[1,1,512]{2,0,1:T(1,128)S(1)}, u32[]{:S(2)}) copy-start(f32[1,1,512]{2,0,1:T(1,128)S(1)} %get-tuple-element.317) | copy-start | bytes 6148
  72.8 146.1 %copy-start.148 = (f32[1,1,512]{2,0,1:T(1,128)}, f32[1,1,512]{2,0,1:T(1,128)S(1)}, u32[]{:S(2)}) copy-start(f32[1,1,512]{2,0,1:T(1,128)S(1)} %get-tuple-element.336) | copy-start | bytes 6148
  72.8 146.1 %copy-start.150 = (f32[1,1,512]{2,0,1:T(1,128)}, f32[1,1,512]{2,0,1:T(1,128)S(1)}, u32[]{:S(2)}) copy-start(f32[1,1,512]{2,0,1:T(1,128)S(1)} %get-tuple-element.337) | copy-start | bytes 6148
  72.8 146.2 %copy-start.152 = (f32[1,1,512]{2,0,1:T(1,128)}, f32[1,1,512]{2,0,1:T(1,128)S(1)}, u32[]{:S(2)}) copy-start(f32[1,1,512]{2,0,1:T(1,128)S(1)} %get-tuple-element.338) | copy-start | bytes 6148
  72.8 146.2 %copy-start.154 = (f32[1,1,512]{2,0,1:T(1,128)}, f32[1,1,512]{2,0,1:T(1,128)S(1)}, u32[]{:S(2)}) copy-start(f32[1,1,512]{2,0,1:T(1,128)S(1)} %get-tuple-element.339) | copy-start | bytes 6148
  72.8 146.2 %copy-start.156 = (f32[1,1,512]{2,0,1:T(1,128)}, f32[1,1,512]{2,0,1:T(1,128)S(1)}, u32[]{:S(2)}) copy-start(f32[1,1,512]{2,0,1:T(1,128)S(1)} %get-tuple-element.340) | copy-start | bytes 6148
  72.8 146.2 %copy-start.158 = (f32[1,1,512]{2,0,1:T(1,128)}, f32[1,1,512]{2,0,1:T(1,128)S(1)}, u32[]{:S(2)}) copy-start(f32[1,1,512]{2,0,1:T(1,128)S(1)} %get-tuple-element.341) | copy-start | bytes 6148
  72.9 146.2 %copy-start.160 = (f32[1,1,512]{2,0,1:T(1,128)}, f32[1,1,512]{2,0,1:T(1,128)S(1)}, u32[]{:S(2)}) copy-start(f32[1,1,512]{2,0,1:T(1,128)S(1)} %get-tuple-element.342) | copy-start | bytes 6148
  72.9 146.2 %copy-start.162 = (f32[1,1,512]{2,0,1:T(1,128)}, f32[1,1,512]{2,0,1:T(1,128)S(1)}, u32[]{:S(2)}) copy-start(f32[1,1,512]{2,0,1:T(1,128)S(1)} %get-tuple-element.343) | copy-start | bytes 6148
  72.9 146.2 %copy-start.164 = (f32[1,1,512]{2,0,1:T(1,128)}, f32[1,1,512]{2,0,1:T(1,128)S(1)}, u32[]{:S(2)}) copy-start(f32[1,1,512]{2,0,1:T(1,128)S(1)} %get-tuple-element.344) | copy-start | bytes 6148
  72.9 146.2 %copy-start.166 = (f32[1,1,512]{2,0,1:T(1,128)}, f32[1,1,512]{2,0,1:T(1,128)S(1)}, u32[]{:S(2)}) copy-start(f32[1,1,512]{2,0,1:T(1,128)S(1)} %get-tuple-element.345) | copy-start | bytes 6148
  72.9 146.2 %copy-start.168 = (f32[1,1,512]{2,0,1:T(1,128)}, f32[1,1,512]{2,0,1:T(1,128)S(1)}, u32[]{:S(2)}) copy-start(f32[1,1,512]{2,0,1:T(1,128)S(1)} %get-tuple-element.346) | copy-start | bytes 6148
  72.9 146.2 %copy-start.170 = (f32[1,1,512]{2,0,1:T(1,128)}, f32[1,1,512]{2,0,1:T(1,128)S(1)}, u32[]{:S(2)}) copy-start(f32[1,1,512]{2,0,1:T(1,128)S(1)} %get-tuple-element.347) | copy-start | bytes 6148
  72.9 146.2 %copy-start.172 = (f32[1,1,512]{2,0,1:T(1,128)}, f32[1,1,512]{2,0,1:T(1,128)S(1)}, u32[]{:S(2)}) copy-start(f32[1,1,512]{2,0,1:T(1,128)S(1)} %get-tuple-element.348) | copy-start | bytes 6148
  72.9 146.2 %copy-start.174 = (f32[1,1,512]{2,0,1:T(1,128)}, f32[1,1,512]{2,0,1:T(1,128)S(1)}, u32[]{:S(2)}) copy-start(f32[1,1,512]{2,0,1:T(1,128)S(1)} %get-tuple-element.349) | copy-start | bytes 6148
  72.9 146.2 %copy-start.176 = (f32[1,1,512]{2,0,1:T(1,128)}, f32[1,1,512]{2,0,1:T(1,128)S(1)}, u32[]{:S(2)}) copy-start(f32[1,1,512]{2,0,1:T(1,128)S(1)} %get-tuple-element.350) | copy-start | bytes 6148
  72.9 146.2 %copy-start.178 = (f32[1,1,512]{2,0,1:T(1,128)}, f32[1,1,512]{2,0,1:T(1,128)S(1)}, u32[]{:S(2)}) copy-start(f32[1,1,512]{2,0,1:T(1,128)S(1)} %get-tuple-element.351) | copy-start | bytes 6148
  74.3 106.8 %copy-start.118 = (f32[1,1,512]{2,0,1:T(1,128)}, f32[1,1,512]{2,0,1:T(1,128)S(1)}, u32[]{:S(2)}) copy-start(f32[1,1,512]{2,0,1:T(1,128)S(1)} %get-tuple-element.372) | copy-start | bytes 6148
  74.3 106.8 %copy-start.232 = (f32[1,1,512]{2,0,1:T(1,128)}, f32[1,1,512]{2,0,1:T(1,128)S(1)}, u32[]{:S(2)}) copy-start(f32[1,1,512]{2,0,1:T(1,128)S(1)} %get-tuple-element.373) | copy-start | bytes 6148
  74.3 110.3 %copy-start.120 = (f32[1,1,512]{2,0,1:T(1,128)}, f32[1,1,512]{2,0,1:T(1,128)S(1)}, u32[]{:S(2)}) copy-start(f32[1,1,512]{2,0,1:T(1,128)S(1)} %get-tuple-element.370) | copy-start | bytes 6148
  78.8 110.9 %copy-start.36 = (bf16[512,512]{0,1:T(8,128)(2,1)}, bf16[512,512]{0,1:T(8,128)(2,1)S(1)}, u32[]{:S(2)}) copy-start(bf16[512,512]{0,1:T(8,128)(2,1)S(1)} %convolution_convert_fusion.11) | copy-start | bytes 1572868
  250.9 46.1 %copy-start.3 = (f32[256,512]{1,0:T(8,128)}, f32[256,512]{1,0:T(8,128)S(1)}, u32[]{:S(2)}) copy-start(f32[256,512]{1,0:T(8,128)S(1)} %get-tuple-element.415) | copy-start | bytes 1572868
  252.9 37.2 %copy-start.98 = (bf16[256,512]{0,1:T(8,128)(2,1)}, bf16[256,512]{0,1:T(8,128)(2,1)S(1)}, u32[]{:S(2)}) copy-start(bf16[256,512]{0,1:T(8,128)(2,1)S(1)} %copy.254) | copy-start | bytes 786436
  254.5 39.7 %copy-start.99 = (bf16[256,512]{0,1:T(8,128)(2,1)}, bf16[256,512]{0,1:T(8,128)(2,1)S(1)}, u32[]{:S(2)}) copy-start(bf16[256,512]{0,1:T(8,128)(2,1)S(1)} %copy.252) | copy-start | bytes 786436
  256.8 33.2 %copy-start.100 = (bf16[256,512]{0,1:T(8,128)(2,1)}, bf16[256,512]{0,1:T(8,128)(2,1)S(1)}, u32[]{:S(2)}) copy-start(bf16[256,512]{0,1:T(8,128)(2,1)S(1)} %copy.253) | copy-start | bytes 786436
  302.7 51.8 %copy-start.14 = (f32[256,512]{1,0:T(8,128)}, f32[256,512]{1,0:T(8,128)S(1)}, u32[]{:S(2)}) copy-start(f32[256,512]{1,0:T(8,128)S(1)} %get-tuple-element.420) | copy-start | bytes 1572868
  320.9 33.6 %copy-start.180 = (f32[512]{0:T(512)}, f32[512]{0:T(512)S(1)}, u32[]{:S(2)}) copy-start(f32[512]{0:T(512)S(1)} %broadcast_divide_fusion.2) | copy-start | bytes 6148
  321.7 32.9 %copy-start.275 = (f32[512]{0:T(512)}, f32[512]{0:T(512)S(1)}, u32[]{:S(2)}) copy-start(f32[512]{0:T(512)S(1)} %add_rsqrt_fusion) | copy-start | bytes 6148
  565.0 200.7 %reduce-scatter.9.cloned.1.call-start = ((), (), s32[]{:S(2)}) async-start(), calls=%async_computation.9 | async-start | bytes 15728640 | tf_op jit(solution)/shard_map/reduce_scatter | solution.py:494
  607.5 236.1 %reduce-scatter.7.cloned.1.call-start = ((), (), s32[]{:S(2)}) async-start(), calls=%async_computation.8 | async-start | bytes 3538944 | tf_op jit(solution)/shard_map/reduce_scatter | solution.py:495
  664.2 101.6 %copy-start.125 = (s32[8]{0:T(128)S(1)}, s32[8]{0:T(128)}, u32[]{:S(2)}) copy-start(s32[8]{0:T(128)} %param.16) | copy-start | bytes 100
  664.2 101.7 %copy-start.115 = (s32[16]{0:T(128)S(1)}, s32[16]{0:T(128)}, u32[]{:S(2)}) copy-start(s32[16]{0:T(128)} %param.15) | copy-start | bytes 196
  664.2 256.5 %reduce-scatter.11.cloned.1.call-start = ((), (), s32[]{:S(2)}) async-start(), calls=%async_computation.10 | async-start | bytes 3538944 | tf_op jit(solution)/shard_map/reduce_scatter | solution.py:495
  765.8 280.4 %all-gather.9.cloned.1.call-start = ((), (), s32[]{:S(2)}) async-start(), calls=%async_computation.11 | async-start | bytes 7077888 | tf_op jit(solution)/shard_map/all_gather | solution.py:528
  843.6 79.0 %slice-start.1 = ((bf16[16,12288]{1,0:T(8,128)(2,1)}), bf16[16,8192]{1,0:T(8,128)(2,1)S(1)}, s32[]{:S(2)}) async-start(bf16[16,12288]{1,0:T(8,128)(2,1)} %reduce-scatter.7.cloned.1.call-done), calls=%async_computation.13 | async-start | bytes 524288 | tf_op jit(solution)/shard_map/slice | solution.py:497
  (269 other events, 1596.4 us)
Sparse Core Ops, SparseCore 0:
  9.6 61.5 all-gather.6
  72.7 105.8 all-gather.4
  565.1 99.0 reduce-scatter.4
  666.6 99.0 reduce-scatter.8
  769.2 74.3 reduce-scatter.6
  847.0 73.6 reduce-scatter.10
  940.5 105.5 all-gather.8

commit v2 on v1

--- a/solution.py
+++ b/solution.py
@@ -49,19 +49,45 @@
     return jnp.stack([jnp.sin(angle), jnp.cos(angle)], axis=-1).reshape(2 * rows, width)
 
 
+def shift_rel_body(full_ref, out_ref):
+    rows, cols = full_ref.shape[1:]
+    out_ref[0] = pltpu.roll(full_ref[0], cols - rows + 1, 1, stride=1, stride_axis=0)[:, :rows]
+
+
 def shift_rel(full):
     heads, rows, cols = full.shape
-    flat = full.reshape(heads, rows * cols)
-    flat = flat[:, rows - 1 : rows - 1 + rows * (cols - 1)]
-    return flat.reshape(heads, rows, cols - 1)[:, :, :rows]
+    return pl.pallas_call(
+        shift_rel_body,
+        grid=(heads,),
+        out_shape=jax.ShapeDtypeStruct((heads, rows, rows), full.dtype),
+        in_specs=[pl.BlockSpec((1, rows, cols), lambda h: (h, 0, 0))],
+        out_specs=pl.BlockSpec((1, rows, rows), lambda h: (h, 0, 0)),
+    )(full)
+
+
+def unshift_rel_body(part_ref, out_ref):
+    rows = part_ref.shape[1]
+    part = part_ref[0].astype(jnp.float32)
+    value = jnp.concatenate([part, jnp.zeros_like(part)], 1)
+    value = pltpu.roll(value, rows - 1, 1)
+    turn = lax.broadcasted_iota(jnp.int32, value.shape, 0)
+    step = 1
+    while step < rows:
+        moved = pltpu.roll(value, 2 * rows - step, 1)
+        value = jnp.where((turn // step) % 2 == 1, moved, value)
+        step *= 2
+    out_ref[0] = value.astype(out_ref.dtype)
 
 
 def unshift_rel(part_grad):
     heads, rows, _ = part_grad.shape
-    widened = jnp.pad(part_grad, ((0, 0), (0, 0), (0, rows - 1)))
-    flat = widened.reshape(heads, rows * (2 * rows - 1))
-    flat = jnp.pad(flat, ((0, 0), (rows - 1, 1)))
-    return flat.reshape(heads, rows, 2 * rows)
+    return pl.pallas_call(
+        unshift_rel_body,
+        grid=(heads,),
+        out_shape=jax.ShapeDtypeStruct((heads, rows, 2 * rows), part_grad.dtype),
+        in_specs=[pl.BlockSpec((1, rows, rows), lambda h: (h, 0, 0))],
+        out_specs=pl.BlockSpec((1, rows, 2 * rows), lambda h: (h, 0, 0)),
+    )(part_grad)
 
 
 def depthwise(glu, kernel):
@@ -382,7 +408,7 @@
         )
 
 
-def muon(moment, grads, weight_low, first):
+def muon(moment, grads, weight_low):
     many, rows, columns = moment.shape
     scale = 0.2 * math.sqrt(max(rows, columns))
     stack = pl.BlockSpec((1, rows, columns), lambda i: (i, 0, 0))
@@ -390,7 +416,7 @@
         partial(muon_body, scale),
         grid=(many,),
         out_shape=[jax.ShapeDtypeStruct(moment.shape, jnp.float32)] * 2,
-        in_specs=[stack, pl.BlockSpec((rows, columns), lambda i: (0, first + i)), stack],
+        in_specs=[stack, pl.BlockSpec((rows, columns), lambda i: (0, i)), stack],
         out_specs=[stack, stack],
         scratch_shapes=[
             pltpu.VMEM((rows, columns), jnp.float32),
@@ -403,6 +429,22 @@
 def slot_order(slots):
     places = jnp.arange(slots.shape[0])
     return jnp.sum(jnp.where(slots[None, :] == places[:, None], places[None, :], 0), 1)
+
+
+def scatter_grads(grads):
+    squares = sum(item.shape[1] == D for item in grads)
+    merged = jnp.concatenate([item.astype(jnp.bfloat16) for item in grads], 1)
+    return merged, squares
+
+
+def scatter_over(merged, axis):
+    return lax.psum_scatter(merged, axis, scatter_dimension=0, tiled=True)
+
+
+def parted(merged, squares):
+    edge = squares * D
+    rows = merged.shape[0]
+    return merged[:, :edge].reshape(rows, squares, D), merged[:, edge:].reshape(rows, 2, -1)
 
 
 def per_device(
@@ -455,6 +497,7 @@
     square_list = [None] * LAYERS
     wide_list = [None] * LAYERS
     vector_list = [None] * LAYERS
+    waiting, landed = [], []
     for depth in reversed(range(LAYERS)):
         mats, wides, vec, first_kept, attend_kept, conv_kept, second_kept, final_pull = saved[depth]
         grad, out_gain, out_shift = final_pull(grad)
@@ -472,6 +515,13 @@
             g_glu_gate,
             g_conv,
         ) = convolution_back(grad, conv_kept, vec, mats[5], mats[6], mats[7], mask, count)
+        merged, squares = scatter_grads([g_glu_value, g_glu_gate, g_conv, up_two, down_two])
+        if landed:
+            grad, merged, arrived = lax.optimization_barrier((grad, merged, landed[-1][0]))
+            landed[-1] = (arrived,) + landed[-1][1:]
+        else:
+            grad, merged = lax.optimization_barrier((grad, merged))
+        waiting.append((scatter_over(merged, "group"), depth, squares))
         (
             grad,
             att_gain,
@@ -485,16 +535,16 @@
             g_out,
             g_pos,
         ) = attention_back(grad, attend_kept, mats[0], mats[1], mats[2], mats[3], table_low, valid)
+        ready, ready_depth, ready_squares = waiting.pop(0)
+        grad, ready = lax.optimization_barrier((grad, ready))
+        landed.append((scatter_over(ready, "dp"), ready_depth, ready_squares))
         grad, ff1_gain, ff1_shift, ff1_bias, up_one, down_one = feed_back(
             grad, first_kept, wides[0], wides[1]
         )
-        layer_grads = [g_query, g_key, g_value, g_out, g_pos, g_glu_value, g_glu_gate, g_conv]
-        layer_grads += [up_one, down_one, up_two, down_two]
-        merged = jnp.concatenate([item.astype(jnp.bfloat16) for item in layer_grads], 1)
-        merged = lax.psum_scatter(merged, "group", scatter_dimension=0, tiled=True)
-        merged = lax.psum_scatter(merged, "dp", scatter_dimension=0, tiled=True)
-        square_list[depth] = merged[:, : 8 * D].reshape(-1, 8, D)
-        wide_list[depth] = merged[:, 8 * D :].reshape(-1, 4, merged.shape[1] // 6)
+        merged, squares = scatter_grads([g_query, g_key, g_value, g_out, g_pos, up_one, down_one])
+        if depth:
+            grad, merged = lax.optimization_barrier((grad, merged))
+        waiting.append((scatter_over(merged, "group"), depth, squares))
         vector_rows = jnp.stack(
             [
                 ff1_gain,
@@ -518,24 +568,32 @@
         )
         vector_list[depth] = jnp.concatenate([vector_rows, g_kernel], 0)
     input_grad = grad[None]
-    square_grad = jnp.concatenate(square_list, 1)[:, slot_order(square_slots)]
-    wide_grad = jnp.concatenate(wide_list, 1)[:, slot_order(wide_slots)]
-    pieces = square_grad.shape[0]
-    owned = jnp.concatenate(
-        [square_grad.reshape(pieces, groups, -1), wide_grad.reshape(pieces, groups, -1)], 2
-    )
-    owned = lax.all_to_all(owned, "group", split_axis=1, concat_axis=0)
-    owned = lax.all_gather(owned, "dp", axis=1)
-    owned = owned.reshape(D, -1)
-    square_moment_new, square_new = muon(square_moment, owned, square_weights, 0)
-    wide_moment_new, wide_new = muon(
-        wide_moment, owned, wide_weights, square_moment.shape[0] * D // wide_moment.shape[2]
-    )
+    for merged, depth, squares in waiting:
+        landed.append((scatter_over(merged, "dp"), depth, squares))
+    for depth in range(LAYERS):
+        parts = [parted(merged, squares) for merged, at, squares in landed if at == depth]
+        square_list[depth] = jnp.concatenate([parts[1][0], parts[0][0]], 1)
+        wide_list[depth] = jnp.concatenate([parts[1][1], parts[0][1]], 1)
     vector_grad = jnp.stack(vector_list)
     layers, vector_rows, width = vectors.shape
     vector_grad = vector_grad.reshape(layers, groups, vector_rows, width).swapaxes(0, 1)
     own_vector = exchange(vector_grad.reshape(groups, layers * vector_rows, width), True, 2)
+    own_vector, square_grad, wide_grad = lax.optimization_barrier(
+        (own_vector, jnp.concatenate(square_list, 1), jnp.concatenate(wide_list, 1))
+    )
     own_vector = own_vector.reshape(vectors.shape)
+    square_grad = square_grad[:, slot_order(square_slots)]
+    wide_grad = wide_grad[:, slot_order(wide_slots)]
+    pieces = square_grad.shape[0]
+    owned = jnp.concatenate(
+        [wide_grad.reshape(pieces, groups, -1), square_grad.reshape(pieces, groups, -1)], 2
+    )
+    owned = lax.all_to_all(owned, "group", split_axis=1, concat_axis=0)
+    edge = wide_moment.shape[0] * wide_moment.shape[2]
+    own_wide = lax.all_gather(owned[:, :, :edge], "dp", axis=1).reshape(D, -1)
+    own_square = lax.all_gather(owned[:, :, edge:], "dp", axis=1).reshape(D, -1)
+    wide_moment_new, wide_new = muon(wide_moment, own_wide, wide_weights)
+    square_moment_new, square_new = muon(square_moment, own_square, square_weights)
     moment_new = adam_first * vector_moment + (1.0 - adam_first) * own_vector
     second_new = adam_second * vector_second + (1.0 - adam_second) * own_vector * own_vector
     first_hat = moment_new / (1.0 - adam_first**STEP)

time: 1140 us -> 1130 us (level)
  local copies, waits for them, and re-layouts: 165 us -> 92.5 us
  matrix products: 193 us -> 252 us
  waiting for transfers between devices: 486 us -> 452 us
  Pallas kernels: 136 us -> 165 us
    reduce_scatter x4 -> x8, waiting for transfers between devices: 312 us -> 264 us  [scatter_over(): return lax.psum_scatter(merged, axis, scatter_dimension=0, tiled=True)]
    reshape x6 -> x4, local copies, waits for them, and re-layouts: 37.9 us -> 0.06 us  [the longest x2 0.04 us: parted(): merged[:, edge:].reshape(rows, 2, -1)]
    pallas_call x0 -> x4, Pallas kernels: none -> 30.8 us  [the longest x2 17.6 us: unshift_rel(): pl.pallas_call(unshift_rel_body, grid=(heads,), out_shape=jax.ShapeDtypeS...]
    dot_general x2, matrix products: 8.84 us -> 31.3 us  [attention_back(): jnp.einsum('hts,shd->thd', d_scores, split_heads(key_low), preferred_elem...]
    dot_general x2, matrix products: 8.67 us -> 30.2 us  [attention_back(): jnp.einsum('hts,thd->shd', d_scores, split_heads(q_con), preferred_elemen...]
    unnamed x641 -> x605, local copies, waits for them, and re-layouts: 50.2 us -> 33.3 us
    all_gather x1 -> x2, waiting for transfers between devices: 73.3 us -> 85.7 us  [the longest x1 43.8 us: per_device(): own_square = lax.all_gather(owned[:, :, edge:], 'dp', axis=1).reshape(D, -1)]
  transfers between devices with their start and end apart: 7 -> 12, of which waited for: 6 -> 8; matrix products, arithmetic and copies ran while one was open for 6% -> 22% of each run, Pallas kernels for 2% -> 7%
where the time goes in v2:
time: 1130 us; the launch traced here: 1110 us
  waiting for transfers between devices  452 us (40%)
  matrix products  252 us (22%)
  Pallas kernels  165 us (15%)
  local copies, waits for them, and re-layouts  92.5 us (8%)
  other arithmetic  65.7 us (6%)
  between operations  65.2 us (6%)
  blocking collectives  21.2 us (2%)
    reduce_scatter x8, waiting for transfers between devices, scatter_over(): return lax.psum_scatter(merged, axis, scatter_dimension=0, tiled=True)  264 us
    all_gather x1, waiting for transfers between devices, per_device(): lax.all_gather(wide_weights, 'group', axis=0, tiled=True)  100 us
    pallas_call x2, Pallas kernels, muon(): pl.pallas_call(partial(muon_body, scale), grid=(many,), out_shape=[jax.Sh...  67.9 us
    pallas_call x5, Pallas kernels, exchange(): pl.pallas_call(partial(exchange_body, n_dp, n_group, reduce), out_shape=j...  66.7 us
    dot_general x22, matrix products, cross_cols(): lax.dot_general(left, right, (((1,), (1,)), ((), ())), preferred_element_...  49.4 us
    dot_general x24, matrix products, product(): return jnp.dot(left, right, preferred_element_type=jnp.float32)  47.6 us
    all_gather x1, waiting for transfers between devices, per_device(): own_square = lax.all_gather(owned[:, :, edge:], 'dp', axis=1).reshape(D, -1)  43.8 us
    all_gather x1, waiting for transfers between devices, per_device(): own_wide = lax.all_gather(owned[:, :, :edge], 'dp', axis=1).reshape(D, -1)  41.9 us
  transfers between devices with their start and end apart: 12, of which 8 were waited for; matrix products, arithmetic and copies ran while one was open for 22% of the time, Pallas kernels for 7%

profile of v2, /device:TPU:0, one launch (start us, length us, event | category | flops | bytes accessed | tf_op | source)
XLA Modules:
  0.0 1114.9 jit_solution(3221497986599120600)
XLA Ops:
  44.4 7.0 all_gather.21
  78.5 100.1 %all-gather.7.cloned.1.call-done = bf16[8,512,2048]{2,1,0:T(8,128)(2,1)} async-done(((bf16[2,512,2048]{2,1,0:T(8,128)(2,1)}), bf16[8,512,2048]{2,1,0:T(8,128)(2,1)}) %all-gather.7.cloned.1.call-update) | async-done | bytes 16777232 | tf_op jit(solution)/shard_map/all_gather | solution.py:473
  181.1 3.2 fusion.362
  194.1 6.6 shard_map.187
  204.8 6.0 convolution_convert_fusion.37
  218.1 3.4 multiply_reduce_fusion.92
  222.8 11.3 %shard_map.188 = f32[8,4,8,128]{3,2,1,0:T(8,128)} custom-call(f32[1,8,128]{2,1,0:T(8,128)} %reshape.1304.x_ref), custom_call_target="tpu_custom_call" | custom-call | tf_op jit(solution)/shard_map/pallas_call | solution.py:304
  239.7 3.2 fusion.366
  246.5 3.2 fusion.367
  260.2 6.6 shard_map.189
  270.9 5.9 convolution_convert_fusion.34
  282.5 3.3 multiply_reduce_fusion.85
  287.4 12.4 %shard_map.190 = f32[8,4,8,128]{3,2,1,0:T(8,128)} custom-call(f32[1,8,128]{2,1,0:T(8,128)} %reshape.1311.x_ref), custom_call_target="tpu_custom_call" | custom-call | tf_op jit(solution)/shard_map/pallas_call | solution.py:304
  306.0 3.2 fusion.371
  314.3 3.4 multiply_reduce_fusion.33
  323.1 11.5 %shard_map.191 = f32[8,4,8,128]{3,2,1,0:T(8,128)} custom-call(f32[1,8,128]{2,1,0:T(8,128)} %reshape.1313.x_ref), custom_call_target="tpu_custom_call" | custom-call | tf_op jit(solution)/shard_map/pallas_call | solution.py:304
  339.2 3.6 broadcast_multiply_fusion.1
  342.8 4.5 broadcast_multiply_fusion
  349.4 6.4 pad_add_fusion.1
  377.9 5.9 convolution_convert_fusion.31
  385.2 7.3 fusion.66.part_ref
  392.5 8.8 shard_map.192
  403.0 15.6 %convolution_bitcast_fusion.3 = f32[256,8,64]{0,2,1:T(8,128)} fusion(bf16[256,8,64]{0,2,1:T(8,128)(2,1)} %bitcast.703, f32[8,256,256]{2,1,0:T(8,128)} %fusion.374, f32[8,256,256]{2,1,0:T(8,128)} %get-tuple-element.444, f32[8,256]{1,0:T(8,128)S(1)} %copy-done.227), kind=kOutput, calls=%fused_computation.129 | convolution fusion | flops 72354048 | bytes 4988928 | tf_op jit(solution)/shard_map/hts,shd->thd/dot_general | solution.py:203
  425.3 15.5 %convolution_convert_fusion.32 = bf16[8,64,256]{2,1,0:T(8,128)(2,1)} fusion(bf16[256,8,64]{0,2,1:T(8,128)(2,1)} %bitcast.701, f32[8,256,256]{2,1,0:T(8,128)} %fusion.374, f32[8,256,256]{2,1,0:T(8,128)} %get-tuple-element.444, f32[8,256]{1,0:T(8,128)S(1)} %copy-done.227), kind=kOutput, calls=%fused_computation.156 | convolution fusion | flops 72485120 | bytes 4726784 | tf_op jit(solution)/shard_map/hts,thd->shd/dot_general | solution.py:206
  460.1 3.3 fusion.13
  463.5 3.1 multiply_reduce_fusion.36
  468.1 3.0 fusion.6
  478.8 3.5 multiply_reduce_fusion.69
  489.4 12.5 %shard_map.193 = f32[8,4,8,128]{3,2,1,0:T(8,128)} custom-call(f32[1,8,128]{2,1,0:T(8,128)} %reshape.1316.x_ref), custom_call_target="tpu_custom_call" | custom-call | tf_op jit(solution)/shard_map/pallas_call | solution.py:304
  529.0 3.5 fusion.8
  538.2 6.9 convolution_convert_fusion.28
  549.4 6.4 fusion.69.part_ref
  555.8 8.8 shard_map.194
  570.0 15.6 %convolution_bitcast_fusion.1 = f32[256,8,64]{0,2,1:T(8,128)} fusion(bf16[256,8,64]{0,2,1:T(8,128)(2,1)} %bitcast.696, f32[8,256,256]{2,1,0:T(8,128)} %fusion.375, f32[8,256,256]{2,1,0:T(8,128)} %get-tuple-element.432, f32[8,256]{1,0:T(8,128)S(1)} %copy-done.225), kind=kOutput, calls=%fused_computation.127 | convolution fusion | flops 72354048 | bytes 4988928 | tf_op jit(solution)/shard_map/hts,shd->thd/dot_general | solution.py:203
  588.8 14.7 %convolution_convert_fusion.29 = bf16[8,64,256]{2,1,0:T(8,128)(2,1)S(1)} fusion(bf16[256,8,64]{0,2,1:T(8,128)(2,1)S(1)} %bitcast.694, f32[8,256,256]{2,1,0:T(8,128)} %fusion.375, f32[8,256,256]{2,1,0:T(8,128)} %get-tuple-element.432, f32[8,256]{1,0:T(8,128)S(1)} %copy-done.225), kind=kOutput, calls=%fused_computation.153 | convolution fusion | flops 72485120 | bytes 4726784 | tf_op jit(solution)/shard_map/hts,thd->shd/dot_general | solution.py:206
  623.4 21.2 %reduce-scatter.19.cloned.1.call-done = bf16[128,5632]{1,0:T(8,128)(2,1)} async-done(((bf16[512,5632]{1,0:T(8,128)(2,1)}), bf16[128,5632]{1,0:T(8,128)(2,1)}) %reduce-scatter.19.cloned.1.call-update) | async-done | bytes 1441808 | tf_op jit(solution)/shard_map/reduce_scatter | solution.py:441
  645.2 64.5 %reduce-scatter.15.cloned.1.call-done = bf16[128,6656]{1,0:T(8,128)(2,1)} async-done(((bf16[512,6656]{1,0:T(8,128)(2,1)}), bf16[128,6656]{1,0:T(8,128)(2,1)}) %reduce-scatter.15.cloned.1.call-update) | async-done | bytes 1703952 | tf_op jit(solution)/shard_map/reduce_scatter | solution.py:441
  719.1 19.0 %shard_map.195 = f32[24,512]{1,0:T(8,128)} custom-call(f32[4,24,512]{2,1,0:T(8,128)} %copy.272.x_ref), custom_call_target="tpu_custom_call" | custom-call | tf_op jit(solution)/shard_map/pallas_call | solution.py:304
  738.1 46.0 %reduce-scatter.23.cloned.1.call-done = bf16[16,6656]{1,0:T(8,128)(2,1)} async-done(((bf16[128,6656]{1,0:T(8,128)(2,1)}), bf16[16,6656]{1,0:T(8,128)(2,1)}) %reduce-scatter.23.cloned.1.call-update) | async-done | bytes 213008 | tf_op jit(solution)/shard_map/reduce_scatter | solution.py:441
  785.9 65.7 %reduce-scatter.21.cloned.1.call-done = bf16[16,5632]{1,0:T(8,128)(2,1)} async-done(((bf16[128,5632]{1,0:T(8,128)(2,1)}), bf16[16,5632]{1,0:T(8,128)(2,1)}) %reduce-scatter.21.cloned.1.call-update) | async-done | bytes 180240 | tf_op jit(solution)/shard_map/reduce_scatter | solution.py:441
  853.3 66.4 %reduce-scatter.17.cloned.1.call-done = bf16[16,6656]{1,0:T(8,128)(2,1)} async-done(((bf16[128,6656]{1,0:T(8,128)(2,1)}), bf16[16,6656]{1,0:T(8,128)(2,1)}) %reduce-scatter.17.cloned.1.call-update) | async-done | bytes 213008 | tf_op jit(solution)/shard_map/reduce_scatter | solution.py:441
  924.8 14.2 %all_to_all.15 = bf16[1,16,4,6144]{3,1,0,2:T(8,128)(2,1)S(1)} all-to-all(bf16[1,16,4,6144]{3,1,0,2:T(8,128)(2,1)S(1)} %copy.288), channel_id=1, replica_groups=mesh['dp'=8,'group'=4] {'group'}, dimensions={2} | all-to-all | bytes 1572864 | tf_op jit(solution)/shard_map/all_to_all | solution.py:591
  943.7 43.8 %all-gather.11.cloned.1.call-done = bf16[4,128,2048]{2,0,1:T(4,128)(2,1)} async-done(((bf16[4,16,2048]{2,0,1:T(4,128)(2,1)}), bf16[4,128,2048]{2,0,1:T(4,128)(2,1)}) %all-gather.11.cloned.1.call-update) | async-done | bytes 2097168 | tf_op jit(solution)/shard_map/all_gather | solution.py:594
  987.5 4.1 copy.290
  991.5 28.5 %shard_map.196 = (f32[4,512,512]{2,1,0:T(8,128)}, f32[4,512,512]{2,1,0:T(8,128)}) custom-call(f32[4,512,512]{2,1,0:T(8,128)} %moment_ref.2, bf16[512,2048]{1,0:T(8,128)(2,1)} %bitcast.675, bf16[4,512,512]{2,1,0:T(8,128)(2,1)} %weight_ref.2), custom_call_target="tpu_custom_call" | custom-call | tf_op jit(solution)/shard_map/pallas_call | solution.py:415
  1020.0 41.9 %all-gather.13.cloned.1.call-done = bf16[4,128,4096]{2,0,1:T(4,128)(2,1)} async-done(((bf16[4,16,4096]{2,0,1:T(4,128)(2,1)}), bf16[4,128,4096]{2,0,1:T(4,128)(2,1)}) %all-gather.13.cloned.1.call-update) | async-done | bytes 4194320 | tf_op jit(solution)/shard_map/all_gather | solution.py:593
  1062.0 6.5 copy.292
  1068.4 39.4 %shard_map.197 = (f32[2,512,2048]{2,1,0:T(8,128)}, f32[2,512,2048]{2,1,0:T(8,128)}) custom-call(f32[2,512,2048]{2,1,0:T(8,128)} %moment_ref.3, bf16[512,4096]{1,0:T(8,128)(2,1)} %bitcast.674, bf16[2,512,2048]{2,1,0:T(8,128)(2,1)} %weight_ref.3), custom_call_target="tpu_custom_call" | custom-call | tf_op jit(solution)/shard_map/pallas_call | solution.py:415
  (918 shorter events, 249.2 us)
Async XLA Ops:
  7.2 68.1 %all-gather.9.cloned.1.call-start = ((), (), s32[]{:S(2)}) async-start(), calls=%async_computation.10 | async-start | bytes 10485760 | tf_op jit(solution)/shard_map/all_gather | solution.py:472
  8.0 170.7 %all-gather.7.cloned.1.call-start = ((), (), s32[]{:S(2)}) async-start(), calls=%async_computation.9 | async-start | bytes 20971520 | tf_op jit(solution)/shard_map/all_gather | solution.py:473
  8.7 448.4 %reduce-scatter.9.cloned.1.call-start = ((), (), s32[]{:S(2)}) async-start(), calls=%async_computation.11 | async-start | bytes 7208960 | tf_op jit(solution)/shard_map/reduce_scatter | solution.py:441
  71.6 109.4 %copy-start.120 = (f32[256]{0:T(256)}, f32[256]{0:T(256)S(1)}, u32[]{:S(2)}) copy-start(f32[256]{0:T(256)S(1)} %broadcast_multiply_fusion.75) | copy-start | bytes 3076
  71.8 109.2 %copy-start.199 = (f32[256]{0:T(256)}, f32[256]{0:T(256)S(1)}, u32[]{:S(2)}) copy-start(f32[256]{0:T(256)S(1)} %fusion.126) | copy-start | bytes 3076
  71.8 109.2 %copy-start.178 = (f32[256]{0:T(256)}, f32[256]{0:T(256)S(1)}, u32[]{:S(2)}) copy-start(f32[256]{0:T(256)S(1)} %fusion.305) | copy-start | bytes 3076
  72.5 144.8 %copy-start.134 = (f32[1,1,512]{2,0,1:T(1,128)}, f32[1,1,512]{2,0,1:T(1,128)S(1)}, u32[]{:S(2)}) copy-start(f32[1,1,512]{2,0,1:T(1,128)S(1)} %get-tuple-element.361) | copy-start | bytes 6148
  72.5 144.8 %copy-start.136 = (f32[1,1,512]{2,0,1:T(1,128)}, f32[1,1,512]{2,0,1:T(1,128)S(1)}, u32[]{:S(2)}) copy-start(f32[1,1,512]{2,0,1:T(1,128)S(1)} %get-tuple-element.362) | copy-start | bytes 6148
  72.5 164.8 %copy-start.132 = (f32[1,1,512]{2,0,1:T(1,128)}, f32[1,1,512]{2,0,1:T(1,128)S(1)}, u32[]{:S(2)}) copy-start(f32[1,1,512]{2,0,1:T(1,128)S(1)} %get-tuple-element.356) | copy-start | bytes 6148
  72.5 206.3 %copy-start.116 = (f32[1,1,512]{2,0,1:T(1,128)}, f32[1,1,512]{2,0,1:T(1,128)S(1)}, u32[]{:S(2)}) copy-start(f32[1,1,512]{2,0,1:T(1,128)S(1)} %get-tuple-element.344) | copy-start | bytes 6148
  73.1 144.2 %copy-start.138 = (f32[1,1,512]{2,0,1:T(1,128)}, f32[1,1,512]{2,0,1:T(1,128)S(1)}, u32[]{:S(2)}) copy-start(f32[1,1,512]{2,0,1:T(1,128)S(1)} %get-tuple-element.363) | copy-start | bytes 6148
  73.1 144.2 %copy-start.140 = (f32[1,1,512]{2,0,1:T(1,128)}, f32[1,1,512]{2,0,1:T(1,128)S(1)}, u32[]{:S(2)}) copy-start(f32[1,1,512]{2,0,1:T(1,128)S(1)} %get-tuple-element.364) | copy-start | bytes 6148
  73.1 144.2 %copy-start.142 = (f32[1,1,512]{2,0,1:T(1,128)}, f32[1,1,512]{2,0,1:T(1,128)S(1)}, u32[]{:S(2)}) copy-start(f32[1,1,512]{2,0,1:T(1,128)S(1)} %get-tuple-element.365) | copy-start | bytes 6148
  73.1 144.2 %copy-start.144 = (f32[1,1,512]{2,0,1:T(1,128)}, f32[1,1,512]{2,0,1:T(1,128)S(1)}, u32[]{:S(2)}) copy-start(f32[1,1,512]{2,0,1:T(1,128)S(1)} %get-tuple-element.366) | copy-start | bytes 6148
  73.1 144.2 %copy-start.146 = (f32[1,1,512]{2,0,1:T(1,128)}, f32[1,1,512]{2,0,1:T(1,128)S(1)}, u32[]{:S(2)}) copy-start(f32[1,1,512]{2,0,1:T(1,128)S(1)} %get-tuple-element.367) | copy-start | bytes 6148
  73.1 144.2 %copy-start.148 = (f32[1,1,512]{2,0,1:T(1,128)}, f32[1,1,512]{2,0,1:T(1,128)S(1)}, u32[]{:S(2)}) copy-start(f32[1,1,512]{2,0,1:T(1,128)S(1)} %get-tuple-element.368) | copy-start | bytes 6148
  73.1 144.2 %copy-start.150 = (f32[1,1,512]{2,0,1:T(1,128)}, f32[1,1,512]{2,0,1:T(1,128)S(1)}, u32[]{:S(2)}) copy-start(f32[1,1,512]{2,0,1:T(1,128)S(1)} %get-tuple-element.369) | copy-start | bytes 6148
  73.2 144.2 %copy-start.152 = (f32[1,1,512]{2,0,1:T(1,128)}, f32[1,1,512]{2,0,1:T(1,128)S(1)}, u32[]{:S(2)}) copy-start(f32[1,1,512]{2,0,1:T(1,128)S(1)} %get-tuple-element.370) | copy-start | bytes 6148
  73.2 144.2 %copy-start.154 = (f32[1,1,512]{2,0,1:T(1,128)}, f32[1,1,512]{2,0,1:T(1,128)S(1)}, u32[]{:S(2)}) copy-start(f32[1,1,512]{2,0,1:T(1,128)S(1)} %get-tuple-element.371) | copy-start | bytes 6148
  73.2 144.2 %copy-start.156 = (f32[1,1,512]{2,0,1:T(1,128)}, f32[1,1,512]{2,0,1:T(1,128)S(1)}, u32[]{:S(2)}) copy-start(f32[1,1,512]{2,0,1:T(1,128)S(1)} %get-tuple-element.372) | copy-start | bytes 6148
  73.2 144.2 %copy-start.158 = (f32[1,1,512]{2,0,1:T(1,128)}, f32[1,1,512]{2,0,1:T(1,128)S(1)}, u32[]{:S(2)}) copy-start(f32[1,1,512]{2,0,1:T(1,128)S(1)} %get-tuple-element.373) | copy-start | bytes 6148
  73.2 144.2 %copy-start.160 = (f32[1,1,512]{2,0,1:T(1,128)}, f32[1,1,512]{2,0,1:T(1,128)S(1)}, u32[]{:S(2)}) copy-start(f32[1,1,512]{2,0,1:T(1,128)S(1)} %get-tuple-element.374) | copy-start | bytes 6148
  73.2 144.2 %copy-start.162 = (f32[1,1,512]{2,0,1:T(1,128)}, f32[1,1,512]{2,0,1:T(1,128)S(1)}, u32[]{:S(2)}) copy-start(f32[1,1,512]{2,0,1:T(1,128)S(1)} %get-tuple-element.375) | copy-start | bytes 6148
  73.2 144.2 %copy-start.164 = (f32[1,1,512]{2,0,1:T(1,128)}, f32[1,1,512]{2,0,1:T(1,128)S(1)}, u32[]{:S(2)}) copy-start(f32[1,1,512]{2,0,1:T(1,128)S(1)} %get-tuple-element.376) | copy-start | bytes 6148
  73.2 144.2 %copy-start.166 = (f32[1,1,512]{2,0,1:T(1,128)}, f32[1,1,512]{2,0,1:T(1,128)S(1)}, u32[]{:S(2)}) copy-start(f32[1,1,512]{2,0,1:T(1,128)S(1)} %get-tuple-element.377) | copy-start | bytes 6148
  73.2 144.2 %copy-start.168 = (f32[1,1,512]{2,0,1:T(1,128)}, f32[1,1,512]{2,0,1:T(1,128)S(1)}, u32[]{:S(2)}) copy-start(f32[1,1,512]{2,0,1:T(1,128)S(1)} %get-tuple-element.378) | copy-start | bytes 6148
  73.2 144.2 %copy-start.170 = (f32[1,1,512]{2,0,1:T(1,128)}, f32[1,1,512]{2,0,1:T(1,128)S(1)}, u32[]{:S(2)}) copy-start(f32[1,1,512]{2,0,1:T(1,128)S(1)} %get-tuple-element.379) | copy-start | bytes 6148
  74.6 106.5 %copy-start.112 = (f32[1,1,512]{2,0,1:T(1,128)}, f32[1,1,512]{2,0,1:T(1,128)S(1)}, u32[]{:S(2)}) copy-start(f32[1,1,512]{2,0,1:T(1,128)S(1)} %get-tuple-element.399) | copy-start | bytes 6148
  74.6 106.5 %copy-start.222 = (f32[1,1,512]{2,0,1:T(1,128)}, f32[1,1,512]{2,0,1:T(1,128)S(1)}, u32[]{:S(2)}) copy-start(f32[1,1,512]{2,0,1:T(1,128)S(1)} %get-tuple-element.400) | copy-start | bytes 6148
  74.6 110.0 %copy-start.114 = (f32[1,1,512]{2,0,1:T(1,128)}, f32[1,1,512]{2,0,1:T(1,128)S(1)}, u32[]{:S(2)}) copy-start(f32[1,1,512]{2,0,1:T(1,128)S(1)} %get-tuple-element.397) | copy-start | bytes 6148
  76.8 180.6 %copy-start.35 = (bf16[512,512]{0,1:T(8,128)(2,1)}, bf16[512,512]{0,1:T(8,128)(2,1)S(1)}, u32[]{:S(2)}) copy-start(bf16[512,512]{0,1:T(8,128)(2,1)S(1)} %convolution_convert_fusion.10) | copy-start | bytes 1572868
  78.5 112.8 %copy-start.33 = (bf16[512,512]{0,1:T(8,128)(2,1)}, bf16[512,512]{0,1:T(8,128)(2,1)S(1)}, u32[]{:S(2)}) copy-start(bf16[512,512]{0,1:T(8,128)(2,1)S(1)} %convolution_convert_fusion.11) | copy-start | bytes 1572868
  250.1 133.7 %copy-start.6 = (bf16[256,512]{1,0:T(8,128)(2,1)}, bf16[256,512]{1,0:T(8,128)(2,1)S(1)}, u32[]{:S(2)}) copy-start(bf16[256,512]{1,0:T(8,128)(2,1)S(1)} %add_convert_fusion.6) | copy-start | bytes 786436
  375.6 159.3 %reduce-scatter.11.cloned.1.call-start = ((), (), s32[]{:S(2)}) async-start(), calls=%async_computation.12 | async-start | bytes 1622016 | tf_op jit(solution)/shard_map/reduce_scatter | solution.py:441
  457.1 156.8 %reduce-scatter.13.cloned.1.call-start = ((), (), s32[]{:S(2)}) async-start(), calls=%async_computation.13 | async-start | bytes 8519680 | tf_op jit(solution)/shard_map/reduce_scatter | solution.py:441
  473.4 171.3 %reduce-scatter.19.cloned.1.call-start = ((), (), s32[]{:S(2)}) async-start(), calls=%async_computation.16 | async-start | bytes 7208960 | tf_op jit(solution)/shard_map/reduce_scatter | solution.py:441
  534.9 174.9 %reduce-scatter.15.cloned.1.call-start = ((), (), s32[]{:S(2)}) async-start(), calls=%async_computation.14 | async-start | bytes 8519680 | tf_op jit(solution)/shard_map/reduce_scatter | solution.py:441
  622.4 87.4 %copy-start.9 = (f32[256,512]{1,0:T(8,128)S(1)}, f32[256,512]{1,0:T(8,128)}, u32[]{:S(2)}) copy-start(f32[256,512]{1,0:T(8,128)} %copy-done.8) | copy-start | bytes 1572868
  622.4 87.4 %copy-start.16 = (f32[256,512]{1,0:T(8,128)S(1)}, f32[256,512]{1,0:T(8,128)}, u32[]{:S(2)}) copy-start(f32[256,512]{1,0:T(8,128)} %copy-done.15) | copy-start | bytes 1572868
  622.4 161.6 %reduce-scatter.23.cloned.1.call-start = ((), (), s32[]{:S(2)}) async-start(), calls=%async_computation.18 | async-start | bytes 1916928 | tf_op jit(solution)/shard_map/reduce_scatter | solution.py:441
  623.2 228.4 %reduce-scatter.21.cloned.1.call-start = ((), (), s32[]{:S(2)}) async-start(), calls=%async_computation.17 | async-start | bytes 1622016 | tf_op jit(solution)/shard_map/reduce_scatter | solution.py:441
  644.9 67.1 %copy-start.11 = (f32[256,512]{1,0:T(8,128)S(1)}, f32[256,512]{1,0:T(8,128)}, u32[]{:S(2)}) copy-start(f32[256,512]{1,0:T(8,128)} %copy-done.10) | copy-start | bytes 1572868
  644.9 67.1 %copy-start.14 = (f32[256,512]{1,0:T(8,128)S(1)}, f32[256,512]{1,0:T(8,128)}, u32[]{:S(2)}) copy-start(f32[256,512]{1,0:T(8,128)} %copy-done.12) | copy-start | bytes 1572868
  644.9 274.8 %reduce-scatter.17.cloned.1.call-start = ((), (), s32[]{:S(2)}) async-start(), calls=%async_computation.15 | async-start | bytes 1916928 | tf_op jit(solution)/shard_map/reduce_scatter | solution.py:441
  709.8 277.7 %all-gather.11.cloned.1.call-start = ((), (), s32[]{:S(2)}) async-start(), calls=%async_computation.19 | async-start | bytes 2359296 | tf_op jit(solution)/shard_map/all_gather | solution.py:594
  716.8 69.0 %slice-start.1 = ((bf16[16,5632]{1,0:T(8,128)(2,1)}), bf16[16,4096]{1,0:T(8,128)(2,1)S(1)}, s32[]{:S(2)}) async-start(bf16[16,5632]{1,0:T(8,128)(2,1)} %reduce-scatter.11.cloned.1.call-done), calls=%async_computation.22 | async-start | bytes 262144 | tf_op jit(solution)/shard_map/slice | solution.py:447
  717.9 135.5 %slice-start = ((bf16[16,5632]{1,0:T(8,128)(2,1)}), bf16[16,1536]{1,0:T(8,128)(2,1)S(1)}, s32[]{:S(2)}) async-start(bf16[16,5632]{1,0:T(8,128)(2,1)} %reduce-scatter.11.cloned.1.call-done), calls=%async_computation.21 | async-start | bytes 98304 | tf_op jit(solution)/shard_map/slice | solution.py:447
  940.0 121.9 %all-gather.13.cloned.1.call-start = ((), (), s32[]{:S(2)}) async-start(), calls=%async_computation.20 | async-start | bytes 4718592 | tf_op jit(solution)/shard_map/all_gather | solution.py:593
  (259 other events, 3206.9 us)
Sparse Core Ops, SparseCore 0:
  9.6 61.5 all-gather.8
  72.7 105.8 all-gather.6
  375.7 55.7 reduce-scatter.8
  457.2 66.0 reduce-scatter.10
  526.4 60.7 reduce-scatter.12
  589.6 54.9 reduce-scatter.18
  647.9 61.8 reduce-scatter.14
  713.2 70.7 reduce-scatter.22
  787.8 63.7 reduce-scatter.20
  855.3 64.3 reduce-scatter.16
  940.1 47.2 all-gather.10
  990.0 71.8 all-gather.12

commit v3 on v1

--- a/solution.py
+++ b/solution.py
@@ -49,11 +49,20 @@
     return jnp.stack([jnp.sin(angle), jnp.cos(angle)], axis=-1).reshape(2 * rows, width)
 
 
+def shift_rel_body(full_ref, out_ref):
+    rows, cols = full_ref.shape[1:]
+    out_ref[0] = pltpu.roll(full_ref[0], cols - rows + 1, 1, stride=1, stride_axis=0)[:, :rows]
+
+
 def shift_rel(full):
     heads, rows, cols = full.shape
-    flat = full.reshape(heads, rows * cols)
-    flat = flat[:, rows - 1 : rows - 1 + rows * (cols - 1)]
-    return flat.reshape(heads, rows, cols - 1)[:, :, :rows]
+    return pl.pallas_call(
+        shift_rel_body,
+        grid=(heads,),
+        out_shape=jax.ShapeDtypeStruct((heads, rows, rows), full.dtype),
+        in_specs=[pl.BlockSpec((1, rows, cols), lambda h: (h, 0, 0))],
+        out_specs=pl.BlockSpec((1, rows, rows), lambda h: (h, 0, 0)),
+    )(full)
 
 
 def unshift_rel(part_grad):
@@ -403,6 +412,14 @@
 def slot_order(slots):
     places = jnp.arange(slots.shape[0])
     return jnp.sum(jnp.where(slots[None, :] == places[:, None], places[None, :], 0), 1)
+
+
+def merge_grads(grads):
+    return jnp.concatenate([item.astype(jnp.bfloat16) for item in grads], 1)
+
+
+def scatter_over(merged, axis):
+    return lax.psum_scatter(merged, axis, scatter_dimension=0, tiled=True)
 
 
 def per_device(
@@ -455,6 +472,7 @@
     square_list = [None] * LAYERS
     wide_list = [None] * LAYERS
     vector_list = [None] * LAYERS
+    waiting, landed = [], []
     for depth in reversed(range(LAYERS)):
         mats, wides, vec, first_kept, attend_kept, conv_kept, second_kept, final_pull = saved[depth]
         grad, out_gain, out_shift = final_pull(grad)
@@ -485,16 +503,21 @@
             g_out,
             g_pos,
         ) = attention_back(grad, attend_kept, mats[0], mats[1], mats[2], mats[3], table_low, valid)
+        if waiting:
+            grad, ready = lax.optimization_barrier((grad, waiting.pop()))
+            landed.append(scatter_over(ready, "dp"))
         grad, ff1_gain, ff1_shift, ff1_bias, up_one, down_one = feed_back(
             grad, first_kept, wides[0], wides[1]
         )
-        layer_grads = [g_query, g_key, g_value, g_out, g_pos, g_glu_value, g_glu_gate, g_conv]
-        layer_grads += [up_one, down_one, up_two, down_two]
-        merged = jnp.concatenate([item.astype(jnp.bfloat16) for item in layer_grads], 1)
-        merged = lax.psum_scatter(merged, "group", scatter_dimension=0, tiled=True)
-        merged = lax.psum_scatter(merged, "dp", scatter_dimension=0, tiled=True)
-        square_list[depth] = merged[:, : 8 * D].reshape(-1, 8, D)
-        wide_list[depth] = merged[:, 8 * D :].reshape(-1, 4, merged.shape[1] // 6)
+        merged = merge_grads(
+            [g_query, g_key, g_value, g_out, g_pos, g_glu_value, g_glu_gate, g_conv]
+            + [up_one, down_one, up_two, down_two]
+        )
+        if depth:
+            grad, merged = lax.optimization_barrier((grad, merged))
+        else:
+            merged, landed[0] = lax.optimization_barrier((merged, landed[0]))
+        waiting.append(scatter_over(merged, "group"))
         vector_rows = jnp.stack(
             [
                 ff1_gain,
@@ -518,24 +541,32 @@
         )
         vector_list[depth] = jnp.concatenate([vector_rows, g_kernel], 0)
     input_grad = grad[None]
-    square_grad = jnp.concatenate(square_list, 1)[:, slot_order(square_slots)]
-    wide_grad = jnp.concatenate(wide_list, 1)[:, slot_order(wide_slots)]
-    pieces = square_grad.shape[0]
-    owned = jnp.concatenate(
-        [square_grad.reshape(pieces, groups, -1), wide_grad.reshape(pieces, groups, -1)], 2
-    )
-    owned = lax.all_to_all(owned, "group", split_axis=1, concat_axis=0)
-    owned = lax.all_gather(owned, "dp", axis=1)
-    owned = owned.reshape(D, -1)
-    square_moment_new, square_new = muon(square_moment, owned, square_weights, 0)
-    wide_moment_new, wide_new = muon(
-        wide_moment, owned, wide_weights, square_moment.shape[0] * D // wide_moment.shape[2]
-    )
+    landed.append(scatter_over(waiting.pop(), "dp"))
+    for depth, merged in enumerate(reversed(landed)):
+        rows = merged.shape[0]
+        square_list[depth] = merged[:, : 8 * D].reshape(rows, 8, D)
+        wide_list[depth] = merged[:, 8 * D :].reshape(rows, 4, -1)
     vector_grad = jnp.stack(vector_list)
     layers, vector_rows, width = vectors.shape
     vector_grad = vector_grad.reshape(layers, groups, vector_rows, width).swapaxes(0, 1)
     own_vector = exchange(vector_grad.reshape(groups, layers * vector_rows, width), True, 2)
+    own_vector, square_grad, wide_grad = lax.optimization_barrier(
+        (own_vector, jnp.concatenate(square_list, 1), jnp.concatenate(wide_list, 1))
+    )
     own_vector = own_vector.reshape(vectors.shape)
+    square_grad = square_grad[:, slot_order(square_slots)]
+    wide_grad = wide_grad[:, slot_order(wide_slots)]
+    pieces = square_grad.shape[0]
+    owned = jnp.concatenate(
+        [wide_grad.reshape(pieces, groups, -1), square_grad.reshape(pieces, groups, -1)], 2
+    )
+    owned = lax.all_to_all(owned, "group", split_axis=1, concat_axis=0)
+    edge = wide_moment.shape[0] * wide_moment.shape[2]
+    owned = lax.all_gather(owned, "dp", axis=1).reshape(D, -1)
+    wide_moment_new, wide_new = muon(wide_moment, owned, wide_weights, 0)
+    square_moment_new, square_new = muon(
+        square_moment, owned, square_weights, edge // D
+    )
     moment_new = adam_first * vector_moment + (1.0 - adam_first) * own_vector
     second_new = adam_second * vector_second + (1.0 - adam_second) * own_vector * own_vector
     first_hat = moment_new / (1.0 - adam_first**STEP)

time: 1140 us -> 1050 us (0.921)
  waiting for transfers between devices: 486 us -> 384 us
  local copies, waits for them, and re-layouts: 165 us -> 102 us
  matrix products: 193 us -> 253 us
  Pallas kernels: 136 us -> 148 us
    reduce_scatter x4, waiting for transfers between devices: 312 us -> 187 us  [scatter_over(): return lax.psum_scatter(merged, axis, scatter_dimension=0, tiled=True)]
    reshape x4 -> x2, local copies, waits for them, and re-layouts: 27.7 us -> 0.06 us  [the longest x1 0.04 us: per_device(): wide_list[depth] = merged[:, 8 * D:].reshape(rows, 4, -1)]
    all_gather x1, waiting for transfers between devices: 73.3 us -> 95.3 us  [per_device(): owned = lax.all_gather(owned, 'dp', axis=1).reshape(D, -1)]
    dot_general x2, matrix products: 8.67 us -> 29.9 us  [attention_back(): jnp.einsum('hts,thd->shd', d_scores, split_heads(q_con), preferred_elemen...]
    dot_general x2, matrix products: 8.84 us -> 30 us  [attention_back(): jnp.einsum('hts,shd->thd', d_scores, split_heads(key_low), preferred_elem...]
    unnamed x641 -> x637, local copies, waits for them, and re-layouts: 50.2 us -> 34.3 us
    pallas_call x0 -> x2, Pallas kernels: none -> 13.2 us  [shift_rel(): pl.pallas_call(shift_rel_body, grid=(heads,), out_shape=jax.ShapeDtypeStr...]
  transfers between devices with their start and end apart: 7 -> 7, of which waited for: 6 -> 5; matrix products, arithmetic and copies ran while one was open for 6% -> 16% of each run, Pallas kernels for 2% -> 3%
where the time goes in v3:
time: 1050 us; the launch traced here: 1030 us
  waiting for transfers between devices  384 us (37%)
  matrix products  253 us (24%)
  Pallas kernels  148 us (14%)
  local copies, waits for them, and re-layouts  102 us (10%)
  between operations  65.2 us (6%)
  other arithmetic  57.9 us (6%)
  blocking collectives  22 us (2%)
    reduce_scatter x4, waiting for transfers between devices, scatter_over(): return lax.psum_scatter(merged, axis, scatter_dimension=0, tiled=True)  187 us
    all_gather x1, waiting for transfers between devices, per_device(): lax.all_gather(wide_weights, 'group', axis=0, tiled=True)  100 us
    all_gather x1, waiting for transfers between devices, per_device(): owned = lax.all_gather(owned, 'dp', axis=1).reshape(D, -1)  95.3 us
    pallas_call x2, Pallas kernels, muon(): pl.pallas_call(partial(muon_body, scale), grid=(many,), out_shape=[jax.Sh...  67.9 us
    pallas_call x5, Pallas kernels, exchange(): pl.pallas_call(partial(exchange_body, n_dp, n_group, reduce), out_shape=j...  66.8 us
    dot_general x22, matrix products, cross_cols(): lax.dot_general(left, right, (((1,), (1,)), ((), ())), preferred_element_...  48.2 us
    dot_general x24, matrix products, product(): return jnp.dot(left, right, preferred_element_type=jnp.float32)  47.9 us
    dot_general x24, matrix products, cross_rows(): lax.dot_general(left, right, (((0,), (0,)), ((), ())), preferred_element_...  37.5 us
  transfers between devices with their start and end apart: 7, of which 5 were waited for; matrix products, arithmetic and copies ran while one was open for 16% of the time, Pallas kernels for 3%

profile of v3, /device:TPU:0, one launch (start us, length us, event | category | flops | bytes accessed | tf_op | source)
XLA Modules:
  0.0 1033.5 jit_solution(1900455549357821464)
XLA Ops:
  44.0 7.0 all_gather.12
  78.2 100.5 %all-gather.5.cloned.1.call-done = bf16[8,512,2048]{2,1,0:T(8,128)(2,1)} async-done(((bf16[2,512,2048]{2,1,0:T(8,128)(2,1)}), bf16[8,512,2048]{2,1,0:T(8,128)(2,1)}) %all-gather.5.cloned.1.call-update) | async-done | bytes 16777232 | tf_op jit(solution)/shard_map/all_gather | solution.py:448
  181.1 3.2 fusion.386
  191.0 2.8 fusion.396.full_ref
  193.8 6.6 shard_map.187
  204.6 4.4 convolution_convert_fusion.35
  216.3 3.2 multiply_reduce_fusion.92
  220.8 11.3 %shard_map.188 = f32[8,4,8,128]{3,2,1,0:T(8,128)} custom-call(f32[1,8,128]{2,1,0:T(8,128)} %reshape.1301.x_ref), custom_call_target="tpu_custom_call" | custom-call | tf_op jit(solution)/shard_map/pallas_call | solution.py:287
  237.7 3.2 fusion.390
  244.4 3.2 fusion.391
  254.7 2.8 fusion.397.full_ref
  257.5 6.6 shard_map.189
  268.2 5.9 convolution_convert_fusion.32
  279.9 3.3 multiply_reduce_fusion.85
  284.6 12.4 %shard_map.190 = f32[8,4,8,128]{3,2,1,0:T(8,128)} custom-call(f32[1,8,128]{2,1,0:T(8,128)} %reshape.1308.x_ref), custom_call_target="tpu_custom_call" | custom-call | tf_op jit(solution)/shard_map/pallas_call | solution.py:287
  303.0 3.2 fusion.395
  308.5 2.9 fusion.12
  311.3 3.4 multiply_reduce_fusion.33
  320.1 11.6 %shard_map.191 = f32[8,4,8,128]{3,2,1,0:T(8,128)} custom-call(f32[1,8,128]{2,1,0:T(8,128)} %reshape.1310.x_ref), custom_call_target="tpu_custom_call" | custom-call | tf_op jit(solution)/shard_map/pallas_call | solution.py:287
  352.5 6.6 convolution_convert_fusion.29
  360.6 7.6 fusion.78
  368.2 14.2 %convolution_convert_fusion.30 = bf16[8,64,256]{2,1,0:T(8,128)(2,1)} fusion(bf16[256,8,64]{0,2,1:T(8,128)(2,1)} %bitcast.716, f32[8,256,256]{2,1,0:T(8,128)S(1)} %fusion.398, f32[8,256,256]{2,1,0:T(8,128)} %get-tuple-element.434, f32[8,256]{1,0:T(8,128)S(1)} %copy-done.231), kind=kOutput, calls=%fused_computation.168 | convolution fusion | flops 72485120 | bytes 4726784 | tf_op jit(solution)/shard_map/hts,thd->shd/dot_general | solution.py:189
  382.5 14.3 %convolution_bitcast_fusion.1 = f32[256,8,64]{0,2,1:T(8,128)} fusion(bf16[256,8,64]{0,2,1:T(8,128)(2,1)} %bitcast.711, f32[8,256,256]{2,1,0:T(8,128)S(1)} %fusion.398, f32[8,256,256]{2,1,0:T(8,128)} %get-tuple-element.434, f32[8,256]{1,0:T(8,128)S(1)} %copy-done.231), kind=kOutput, calls=%fused_computation.141 | convolution fusion | flops 72354048 | bytes 4988928 | tf_op jit(solution)/shard_map/hts,shd->thd/dot_general | solution.py:186
  406.2 4.8 reshape.1430
  411.0 5.1 reshape.1313
  434.0 3.7 fusion.13
  437.7 3.1 multiply_reduce_fusion.36
  449.5 3.0 fusion.4
  465.1 4.0 multiply_reduce_fusion.69
  472.6 12.4 %shard_map.192 = f32[8,4,8,128]{3,2,1,0:T(8,128)} custom-call(f32[1,8,128]{2,1,0:T(8,128)} %reshape.1315.x_ref), custom_call_target="tpu_custom_call" | custom-call | tf_op jit(solution)/shard_map/pallas_call | solution.py:287
  502.2 7.7 fusion.81
  511.4 4.8 reshape.1432
  516.2 5.1 reshape.1318
  523.6 6.7 convolution_convert_fusion.26
  530.3 2.7 fusion.399
  533.0 15.7 %convolution_convert_fusion.27 = bf16[8,64,256]{2,1,0:T(8,128)(2,1)} fusion(bf16[256,8,64]{0,2,1:T(8,128)(2,1)} %bitcast.709, f32[8,256,256]{2,1,0:T(8,128)} %fusion.399, f32[8,256,256]{2,1,0:T(8,128)} %get-tuple-element.422, f32[8,256]{1,0:T(8,128)S(1)} %copy-done.229), kind=kOutput, calls=%fused_computation.165 | convolution fusion | flops 72485120 | bytes 4726784 | tf_op jit(solution)/shard_map/hts,thd->shd/dot_general | solution.py:189
  548.7 15.7 %convolution_bitcast_fusion = f32[256,8,64]{0,2,1:T(8,128)} fusion(bf16[256,8,64]{0,2,1:T(8,128)(2,1)S(1)} %bitcast.704, f32[8,256,256]{2,1,0:T(8,128)} %fusion.399, f32[8,256,256]{2,1,0:T(8,128)} %get-tuple-element.422, f32[8,256]{1,0:T(8,128)S(1)} %copy-done.229), kind=kOutput, calls=%fused_computation.140 | convolution fusion | flops 72354048 | bytes 4988928 | tf_op jit(solution)/shard_map/hts,shd->thd/dot_general | solution.py:186
  612.0 3.1 fusion.10
  617.3 29.8 %reduce-scatter.7.cloned.1.call-done = bf16[16,12288]{1,0:T(8,128)(2,1)} async-done(((bf16[128,12288]{1,0:T(8,128)(2,1)}), bf16[16,12288]{1,0:T(8,128)(2,1)}) %reduce-scatter.7.cloned.1.call-update) | async-done | bytes 393232 | tf_op jit(solution)/shard_map/reduce_scatter | solution.py:422
  647.2 100.6 %reduce-scatter.9.cloned.1.call-done = bf16[128,12288]{1,0:T(8,128)(2,1)} async-done(((bf16[512,12288]{1,0:T(8,128)(2,1)}), bf16[128,12288]{1,0:T(8,128)(2,1)}) %reduce-scatter.9.cloned.1.call-update) | async-done | bytes 3145744 | tf_op jit(solution)/shard_map/reduce_scatter | solution.py:422
  753.1 2.8 fusion.355
  758.6 19.1 %shard_map.193 = f32[24,512]{1,0:T(8,128)} custom-call(f32[4,24,512]{2,1,0:T(8,128)} %copy.252.x_ref), custom_call_target="tpu_custom_call" | custom-call | tf_op jit(solution)/shard_map/pallas_call | solution.py:287
  777.7 56.8 %reduce-scatter.11.cloned.1.call-done = bf16[16,12288]{1,0:T(8,128)(2,1)} async-done(((bf16[128,12288]{1,0:T(8,128)(2,1)}), bf16[16,12288]{1,0:T(8,128)(2,1)}) %reduce-scatter.11.cloned.1.call-update) | async-done | bytes 393232 | tf_op jit(solution)/shard_map/reduce_scatter | solution.py:422
  839.7 15.0 %all_to_all.15 = bf16[1,16,4,6144]{3,1,0,2:T(8,128)(2,1)} all-to-all(bf16[1,16,4,6144]{3,1,0,2:T(8,128)(2,1)S(1)} %copy.267), channel_id=1, replica_groups=mesh['dp'=8,'group'=4] {'group'}, dimensions={2} | all-to-all | bytes 1572864 | tf_op jit(solution)/shard_map/all_to_all | solution.py:563
  856.9 95.3 %all-gather.9.cloned.1.call-done = bf16[4,8,16,1,6144]{4,2,3,0,1:T(8,128)(2,1)} async-done(((bf16[4,1,16,1,6144]{4,2,3,0,1:T(8,128)(2,1)}), bf16[4,8,16,1,6144]{4,2,3,0,1:T(8,128)(2,1)}) %all-gather.9.cloned.1.call-update) | async-done | bytes 6291472 | tf_op jit(solution)/shard_map/all_gather | solution.py:565
  952.2 6.2 copy.269
  958.4 28.5 %shard_map.194 = (f32[4,512,512]{2,1,0:T(8,128)}, f32[4,512,512]{2,1,0:T(8,128)}) custom-call(f32[4,512,512]{2,1,0:T(8,128)} %moment_ref.2, bf16[512,6144]{1,0:T(8,128)(2,1)} %bitcast.681, bf16[4,512,512]{2,1,0:T(8,128)(2,1)} %weight_ref.2), custom_call_target="tpu_custom_call" | custom-call | tf_op jit(solution)/shard_map/pallas_call | solution.py:398
  986.9 39.4 %shard_map.195 = (f32[2,512,2048]{2,1,0:T(8,128)}, f32[2,512,2048]{2,1,0:T(8,128)}) custom-call(f32[2,512,2048]{2,1,0:T(8,128)} %moment_ref.3, bf16[512,6144]{1,0:T(8,128)(2,1)} %bitcast.682, bf16[2,512,2048]{2,1,0:T(8,128)(2,1)} %weight_ref.3), custom_call_target="tpu_custom_call" | custom-call | tf_op jit(solution)/shard_map/pallas_call | solution.py:398
  (928 shorter events, 237.0 us)
Async XLA Ops:
  7.2 67.1 %all-gather.7.cloned.1.call-start = ((), (), s32[]{:S(2)}) async-start(), calls=%async_computation.6 | async-start | bytes 10485760 | tf_op jit(solution)/shard_map/all_gather | solution.py:447
  7.9 32.4 %copy-start.302 = (s32[32]{0:T(128)S(1)}, s32[32]{0:T(128)}, u32[]{:S(2)}) copy-start(s32[32]{0:T(128)} %param.14) | copy-start | bytes 388
  7.9 36.0 %copy-start.106 = (f32[2,12,512]{2,0,1:T(2,128)S(1)}, f32[2,12,512]{2,0,1:T(2,128)}, u32[]{:S(2)}) copy-start(f32[2,12,512]{2,0,1:T(2,128)} %param.19) | copy-start | bytes 147460
  8.0 170.7 %all-gather.5.cloned.1.call-start = ((), (), s32[]{:S(2)}) async-start(), calls=%async_computation.5 | async-start | bytes 20971520 | tf_op jit(solution)/shard_map/all_gather | solution.py:448
  8.7 62.3 %copy-start.26 = (bf16[1,256,512]{2,1,0:T(8,128)(2,1)S(1)}, bf16[1,256,512]{2,1,0:T(8,128)(2,1)}, u32[]{:S(2)}) copy-start(bf16[1,256,512]{2,1,0:T(8,128)(2,1)} %param.12) | copy-start | bytes 786436
  8.7 563.7 %reduce-scatter.5.cloned.1.call-start = ((), (), s32[]{:S(2)}) async-start(), calls=%async_computation.7 | async-start | bytes 15728640 | tf_op jit(solution)/shard_map/reduce_scatter | solution.py:422
  71.1 109.9 %copy-start.121 = (f32[256]{0:T(256)}, f32[256]{0:T(256)S(1)}, u32[]{:S(2)}) copy-start(f32[256]{0:T(256)S(1)} %broadcast_multiply_fusion.75) | copy-start | bytes 3076
  71.3 109.7 %copy-start.204 = (f32[256]{0:T(256)}, f32[256]{0:T(256)S(1)}, u32[]{:S(2)}) copy-start(f32[256]{0:T(256)S(1)} %fusion.150) | copy-start | bytes 3076
  71.4 109.7 %copy-start.186 = (f32[256]{0:T(256)}, f32[256]{0:T(256)S(1)}, u32[]{:S(2)}) copy-start(f32[256]{0:T(256)S(1)} %fusion.329) | copy-start | bytes 3076
  72.0 143.5 %copy-start.135 = (f32[1,1,512]{2,0,1:T(1,128)}, f32[1,1,512]{2,0,1:T(1,128)S(1)}, u32[]{:S(2)}) copy-start(f32[1,1,512]{2,0,1:T(1,128)S(1)} %get-tuple-element.351) | copy-start | bytes 6148
  72.0 143.5 %copy-start.137 = (f32[1,1,512]{2,0,1:T(1,128)}, f32[1,1,512]{2,0,1:T(1,128)S(1)}, u32[]{:S(2)}) copy-start(f32[1,1,512]{2,0,1:T(1,128)S(1)} %get-tuple-element.352) | copy-start | bytes 6148
  72.0 163.2 %copy-start.133 = (f32[1,1,512]{2,0,1:T(1,128)}, f32[1,1,512]{2,0,1:T(1,128)S(1)}, u32[]{:S(2)}) copy-start(f32[1,1,512]{2,0,1:T(1,128)S(1)} %get-tuple-element.346) | copy-start | bytes 6148
  72.0 204.0 %copy-start.117 = (f32[1,1,512]{2,0,1:T(1,128)}, f32[1,1,512]{2,0,1:T(1,128)S(1)}, u32[]{:S(2)}) copy-start(f32[1,1,512]{2,0,1:T(1,128)S(1)} %get-tuple-element.334) | copy-start | bytes 6148
  72.1 143.4 %copy-start.139 = (f32[1,1,512]{2,0,1:T(1,128)}, f32[1,1,512]{2,0,1:T(1,128)S(1)}, u32[]{:S(2)}) copy-start(f32[1,1,512]{2,0,1:T(1,128)S(1)} %get-tuple-element.353) | copy-start | bytes 6148
  72.1 143.4 %copy-start.141 = (f32[1,1,512]{2,0,1:T(1,128)}, f32[1,1,512]{2,0,1:T(1,128)S(1)}, u32[]{:S(2)}) copy-start(f32[1,1,512]{2,0,1:T(1,128)S(1)} %get-tuple-element.354) | copy-start | bytes 6148
  72.1 143.4 %copy-start.143 = (f32[1,1,512]{2,0,1:T(1,128)}, f32[1,1,512]{2,0,1:T(1,128)S(1)}, u32[]{:S(2)}) copy-start(f32[1,1,512]{2,0,1:T(1,128)S(1)} %get-tuple-element.355) | copy-start | bytes 6148
  72.1 143.4 %copy-start.145 = (f32[1,1,512]{2,0,1:T(1,128)}, f32[1,1,512]{2,0,1:T(1,128)S(1)}, u32[]{:S(2)}) copy-start(f32[1,1,512]{2,0,1:T(1,128)S(1)} %get-tuple-element.356) | copy-start | bytes 6148
  72.1 143.4 %copy-start.147 = (f32[1,1,512]{2,0,1:T(1,128)}, f32[1,1,512]{2,0,1:T(1,128)S(1)}, u32[]{:S(2)}) copy-start(f32[1,1,512]{2,0,1:T(1,128)S(1)} %get-tuple-element.357) | copy-start | bytes 6148
  72.1 143.4 %copy-start.149 = (f32[1,1,512]{2,0,1:T(1,128)}, f32[1,1,512]{2,0,1:T(1,128)S(1)}, u32[]{:S(2)}) copy-start(f32[1,1,512]{2,0,1:T(1,128)S(1)} %get-tuple-element.358) | copy-start | bytes 6148
  72.1 143.4 %copy-start.151 = (f32[1,1,512]{2,0,1:T(1,128)}, f32[1,1,512]{2,0,1:T(1,128)S(1)}, u32[]{:S(2)}) copy-start(f32[1,1,512]{2,0,1:T(1,128)S(1)} %get-tuple-element.359) | copy-start | bytes 6148
  72.2 143.4 %copy-start.153 = (f32[1,1,512]{2,0,1:T(1,128)}, f32[1,1,512]{2,0,1:T(1,128)S(1)}, u32[]{:S(2)}) copy-start(f32[1,1,512]{2,0,1:T(1,128)S(1)} %get-tuple-element.360) | copy-start | bytes 6148
  72.2 143.4 %copy-start.155 = (f32[1,1,512]{2,0,1:T(1,128)}, f32[1,1,512]{2,0,1:T(1,128)S(1)}, u32[]{:S(2)}) copy-start(f32[1,1,512]{2,0,1:T(1,128)S(1)} %get-tuple-element.361) | copy-start | bytes 6148
  72.2 143.4 %copy-start.157 = (f32[1,1,512]{2,0,1:T(1,128)}, f32[1,1,512]{2,0,1:T(1,128)S(1)}, u32[]{:S(2)}) copy-start(f32[1,1,512]{2,0,1:T(1,128)S(1)} %get-tuple-element.362) | copy-start | bytes 6148
  72.2 143.4 %copy-start.159 = (f32[1,1,512]{2,0,1:T(1,128)}, f32[1,1,512]{2,0,1:T(1,128)S(1)}, u32[]{:S(2)}) copy-start(f32[1,1,512]{2,0,1:T(1,128)S(1)} %get-tuple-element.363) | copy-start | bytes 6148
  72.2 143.4 %copy-start.161 = (f32[1,1,512]{2,0,1:T(1,128)}, f32[1,1,512]{2,0,1:T(1,128)S(1)}, u32[]{:S(2)}) copy-start(f32[1,1,512]{2,0,1:T(1,128)S(1)} %get-tuple-element.364) | copy-start | bytes 6148
  72.2 143.4 %copy-start.163 = (f32[1,1,512]{2,0,1:T(1,128)}, f32[1,1,512]{2,0,1:T(1,128)S(1)}, u32[]{:S(2)}) copy-start(f32[1,1,512]{2,0,1:T(1,128)S(1)} %get-tuple-element.365) | copy-start | bytes 6148
  72.2 143.4 %copy-start.165 = (f32[1,1,512]{2,0,1:T(1,128)}, f32[1,1,512]{2,0,1:T(1,128)S(1)}, u32[]{:S(2)}) copy-start(f32[1,1,512]{2,0,1:T(1,128)S(1)} %get-tuple-element.366) | copy-start | bytes 6148
  72.2 143.4 %copy-start.167 = (f32[1,1,512]{2,0,1:T(1,128)}, f32[1,1,512]{2,0,1:T(1,128)S(1)}, u32[]{:S(2)}) copy-start(f32[1,1,512]{2,0,1:T(1,128)S(1)} %get-tuple-element.367) | copy-start | bytes 6148
  72.2 143.4 %copy-start.169 = (f32[1,1,512]{2,0,1:T(1,128)}, f32[1,1,512]{2,0,1:T(1,128)S(1)}, u32[]{:S(2)}) copy-start(f32[1,1,512]{2,0,1:T(1,128)S(1)} %get-tuple-element.368) | copy-start | bytes 6148
  72.2 143.4 %copy-start.171 = (f32[1,1,512]{2,0,1:T(1,128)}, f32[1,1,512]{2,0,1:T(1,128)S(1)}, u32[]{:S(2)}) copy-start(f32[1,1,512]{2,0,1:T(1,128)S(1)} %get-tuple-element.369) | copy-start | bytes 6148
  72.3 143.4 %copy-start.173 = (f32[1,1,512]{2,0,1:T(1,128)}, f32[1,1,512]{2,0,1:T(1,128)S(1)}, u32[]{:S(2)}) copy-start(f32[1,1,512]{2,0,1:T(1,128)S(1)} %get-tuple-element.370) | copy-start | bytes 6148
  72.3 143.4 %copy-start.175 = (f32[1,1,512]{2,0,1:T(1,128)}, f32[1,1,512]{2,0,1:T(1,128)S(1)}, u32[]{:S(2)}) copy-start(f32[1,1,512]{2,0,1:T(1,128)S(1)} %get-tuple-element.371) | copy-start | bytes 6148
  73.6 107.5 %copy-start.113 = (f32[1,1,512]{2,0,1:T(1,128)}, f32[1,1,512]{2,0,1:T(1,128)S(1)}, u32[]{:S(2)}) copy-start(f32[1,1,512]{2,0,1:T(1,128)S(1)} %get-tuple-element.389) | copy-start | bytes 6148
  73.6 107.5 %copy-start.226 = (f32[1,1,512]{2,0,1:T(1,128)}, f32[1,1,512]{2,0,1:T(1,128)S(1)}, u32[]{:S(2)}) copy-start(f32[1,1,512]{2,0,1:T(1,128)S(1)} %get-tuple-element.390) | copy-start | bytes 6148
  73.6 111.0 %copy-start.115 = (f32[1,1,512]{2,0,1:T(1,128)}, f32[1,1,512]{2,0,1:T(1,128)S(1)}, u32[]{:S(2)}) copy-start(f32[1,1,512]{2,0,1:T(1,128)S(1)} %get-tuple-element.387) | copy-start | bytes 6148
  73.6 142.1 %copy-start.177 = (f32[1,1,512]{2,0,1:T(1,128)}, f32[1,1,512]{2,0,1:T(1,128)S(1)}, u32[]{:S(2)}) copy-start(f32[1,1,512]{2,0,1:T(1,128)S(1)} %get-tuple-element.382) | copy-start | bytes 6148
  78.1 112.9 %copy-start.32 = (bf16[512,512]{0,1:T(8,128)(2,1)}, bf16[512,512]{0,1:T(8,128)(2,1)S(1)}, u32[]{:S(2)}) copy-start(bf16[512,512]{0,1:T(8,128)(2,1)S(1)} %convolution_convert_fusion.11) | copy-start | bytes 1572868
  279.9 53.5 %copy-start.13 = (f32[256,512]{1,0:T(8,128)}, f32[256,512]{1,0:T(8,128)S(1)}, u32[]{:S(2)}) copy-start(f32[256,512]{1,0:T(8,128)S(1)} %get-tuple-element.437) | copy-start | bytes 1572868
  459.7 187.4 %reduce-scatter.7.cloned.1.call-start = ((), (), s32[]{:S(2)}) async-start(), calls=%async_computation.8 | async-start | bytes 3538944 | tf_op jit(solution)/shard_map/reduce_scatter | solution.py:422
  572.5 175.3 %reduce-scatter.9.cloned.1.call-start = ((), (), s32[]{:S(2)}) async-start(), calls=%async_computation.9 | async-start | bytes 15728640 | tf_op jit(solution)/shard_map/reduce_scatter | solution.py:422
  647.1 101.3 %copy-start.120 = (s32[8]{0:T(128)S(1)}, s32[8]{0:T(128)}, u32[]{:S(2)}) copy-start(s32[8]{0:T(128)} %param.16) | copy-start | bytes 100
  647.1 101.4 %copy-start.110 = (s32[16]{0:T(128)S(1)}, s32[16]{0:T(128)}, u32[]{:S(2)}) copy-start(s32[16]{0:T(128)} %param.15) | copy-start | bytes 196
  647.1 101.7 %copy-start.7 = (f32[256,512]{1,0:T(8,128)S(1)}, f32[256,512]{1,0:T(8,128)}, u32[]{:S(2)}) copy-start(f32[256,512]{1,0:T(8,128)} %copy-done.6) | copy-start | bytes 1572868
  647.1 101.7 %copy-start.14 = (f32[256,512]{1,0:T(8,128)S(1)}, f32[256,512]{1,0:T(8,128)}, u32[]{:S(2)}) copy-start(f32[256,512]{1,0:T(8,128)} %copy-done.13) | copy-start | bytes 1572868
  647.1 187.3 %reduce-scatter.11.cloned.1.call-start = ((), (), s32[]{:S(2)}) async-start(), calls=%async_computation.10 | async-start | bytes 3538944 | tf_op jit(solution)/shard_map/reduce_scatter | solution.py:422
  748.1 204.0 %all-gather.9.cloned.1.call-start = ((), (), s32[]{:S(2)}) async-start(), calls=%async_computation.11 | async-start | bytes 7077888 | tf_op jit(solution)/shard_map/all_gather | solution.py:565
  756.3 79.1 %slice-start = ((bf16[16,12288]{1,0:T(8,128)(2,1)}), bf16[16,4096]{1,0:T(8,128)(2,1)S(1)}, s32[]{:S(2)}) async-start(bf16[16,12288]{1,0:T(8,128)(2,1)} %reduce-scatter.7.cloned.1.call-done), calls=%async_computation.12 | async-start | bytes 262144 | tf_op jit(solution)/shard_map/slice | solution.py:547
  757.7 78.8 %slice-start.1 = ((bf16[16,12288]{1,0:T(8,128)(2,1)}), bf16[16,8192]{1,0:T(8,128)(2,1)S(1)}, s32[]{:S(2)}) async-start(bf16[16,12288]{1,0:T(8,128)(2,1)} %reduce-scatter.7.cloned.1.call-done), calls=%async_computation.13 | async-start | bytes 524288 | tf_op jit(solution)/shard_map/slice | solution.py:548
  (269 other events, 1218.2 us)
Sparse Core Ops, SparseCore 0:
  9.6 61.5 all-gather.6
  72.7 105.8 all-gather.4
  459.8 99.8 reduce-scatter.4
  572.6 74.4 reduce-scatter.6
  649.5 98.2 reduce-scatter.8
  751.2 83.2 reduce-scatter.10
  854.9 97.2 all-gather.8
